TPU v7x, 256 devices: a whole 4x4x8 slice. The times are simulated.
256 devices in a mesh: prefix: 8 (over z_hi, core), replica: 8 (over z_lo, x), tensor: 4 (over y).
Axes of the slice: x: 4, y: 4, z: 8 (z_hi: 4, z_lo: 2; z = z_hi * 2 + z_lo), core: 2. Of those that a mesh axis runs over, the one named last changes fastest.
Arguments:
- queries: bfloat16 [4, 64, 8192], P(None, ('prefix', 'replica'), 'tensor'), may hold values from -8 to 8
- common_prefix_keys: bfloat16 [196608, 1024], P(('prefix', 'replica'), 'tensor'), may hold values from -12 to 12
- common_prefix_values: bfloat16 [196608, 1024], P(('prefix', 'replica'), 'tensor'), may hold values from -6 to 6
- branch_suffix_keys: bfloat16 [64, 1024, 1024], P(('prefix', 'replica'), None, 'tensor'), may hold values from -12 to 12
- branch_suffix_values: bfloat16 [64, 1024, 1024], P(('prefix', 'replica'), None, 'tensor'), may hold values from -6 to 6
- position_keys: bfloat16 [4, 64, 1024], P(None, ('prefix', 'replica'), 'tensor'), may hold values from -12 to 12
- position_values: bfloat16 [4, 64, 1024], P(None, ('prefix', 'replica'), 'tensor'), may hold values from -6 to 6
- lengths: int32 [64], P(('prefix', 'replica')), may hold values from 1 to 1024, 32768 in all
- out_weight: bfloat16 [8192, 5120], P('tensor', ('prefix', 'replica')), may hold values from -0.0625 to 0.0625
Outputs:
- projected: bfloat16 [4, 64, 5120], P(None, 'tensor', ('prefix', 'replica'))
Inputs may be any that keep to these rules, and one draw needn't show every extreme that they name: The lengths sum to 32768 and the largest is exactly 1024.
All inputs are finite; a program needn't handle non-finite values. No bound on the sum of `lengths` on one device may be relied on, other than what follows from the above.
Results may differ from a plain program's by a relative error of at most 0.015.
Values may be sent and summed in bfloat16 or wider, within the bound.
No kernel may reach another device: no remote copies, remote signals or barrier semaphores. Data moves between devices by JAX's collectives and lax.ppermute only.
A program may use at most 64 MiB of HBM per device.

v0:
```python
import jax
import jax.numpy as jnp
from jax import lax
from jax.sharding import PartitionSpec as P

QUERY_HEADS = 64
KEY_VALUE_HEADS = 8
HEAD_SIZE = 128


def local(
    queries,
    common_prefix_keys,
    common_prefix_values,
    branch_suffix_keys,
    branch_suffix_values,
    position_keys,
    position_values,
    lengths,
    out_weight,
):
    query_group_width = QUERY_HEADS // KEY_VALUE_HEADS
    score_scale = HEAD_SIZE ** (-0.5)
    kv_local = common_prefix_keys.shape[1] // HEAD_SIZE
    heads_local = kv_local * query_group_width
    row_width = queries.shape[2]
    steps_count = queries.shape[0]
    branch_local = queries.shape[1]
    n_prefix = lax.axis_size("prefix")
    n_replica = lax.axis_size("replica")
    everyone = lax.all_gather(queries, ("prefix", "replica"), axis=1, tiled=True)
    branch_all = everyone.shape[1]
    number_of_rows = steps_count * branch_all
    query_all = everyone.reshape(number_of_rows, kv_local, query_group_width, HEAD_SIZE)
    pre_rows = common_prefix_keys.shape[0]
    key_span = min(512, pre_rows)
    blocked_keys = common_prefix_keys.reshape(pre_rows // key_span, key_span, kv_local, HEAD_SIZE)
    blocked_values = common_prefix_values.reshape(
        pre_rows // key_span, key_span, kv_local, HEAD_SIZE
    )

    def prefix_step(state_carry, kv_block):
        run_max, run_total, run_sum = state_carry
        keys_blk, values_blk = kv_block
        scores = (
            jnp.einsum("rgqd,kgd->rgqk", query_all, keys_blk, preferred_element_type=jnp.float32)
            * score_scale
        )
        new_max = jnp.maximum(run_max, jnp.max(scores, axis=-1))
        rescale = jnp.exp(run_max - new_max)
        weights = jnp.exp(scores - new_max[..., None])
        run_total = run_total * rescale + jnp.sum(weights, axis=-1)
        run_sum = run_sum * rescale[..., None] + jnp.einsum(
            "rgqk,kgd->rgqd",
            weights.astype(jnp.bfloat16),
            values_blk,
            preferred_element_type=jnp.float32,
        )
        return ((new_max, run_total, run_sum), None)

    initial_state = (
        jnp.full((number_of_rows, kv_local, query_group_width), -jnp.inf, jnp.float32),
        jnp.zeros((number_of_rows, kv_local, query_group_width), jnp.float32),
        jnp.zeros((number_of_rows, kv_local, query_group_width, HEAD_SIZE), jnp.float32),
    )
    (prefix_maximum, prefix_weighted_total, prefix_exp_sum), unused = lax.scan(
        prefix_step, initial_state, (blocked_keys, blocked_values)
    )
    part_out = prefix_exp_sum / prefix_weighted_total[..., None]
    part_lse = prefix_maximum + jnp.log(prefix_weighted_total)
    query_own = queries.reshape(steps_count, branch_local, kv_local, query_group_width, HEAD_SIZE)
    recent_keys = position_keys.reshape(steps_count, branch_local, kv_local, HEAD_SIZE)
    recent_values = position_values.reshape(steps_count, branch_local, kv_local, HEAD_SIZE)
    fresh_scores = (
        jnp.einsum("pbgqd,jbgd->pbgqj", query_own, recent_keys, preferred_element_type=jnp.float32)
        * score_scale
    )
    causal = (
        jnp.arange(steps_count, dtype=jnp.int32)[None, :]
        <= jnp.arange(steps_count, dtype=jnp.int32)[:, None]
    )
    fresh_scores = jnp.where(causal[:, None, None, None, :], fresh_scores, -jnp.inf)
    own_max = jnp.max(fresh_scores, axis=-1)
    fresh_weights = jnp.exp(fresh_scores - own_max[..., None])
    own_total = jnp.sum(fresh_weights, axis=-1)
    own_sum = jnp.einsum(
        "pbgqj,jbgd->pbgqd",
        fresh_weights.astype(jnp.bfloat16),
        recent_values,
        preferred_element_type=jnp.float32,
    )
    suffix_slots = branch_suffix_keys.shape[1]
    suffix_span = min(512, suffix_slots)
    stored_keys = branch_suffix_keys.reshape(branch_local, suffix_slots, kv_local, HEAD_SIZE)
    stored_values = branch_suffix_values.reshape(branch_local, suffix_slots, kv_local, HEAD_SIZE)
    block_limit = (jnp.max(lengths) + suffix_span - 1) // suffix_span

    def suffix_step(block_index, state_carry):
        run_max, run_total, run_sum = state_carry
        block_start = block_index * suffix_span
        keys_blk = lax.dynamic_slice_in_dim(stored_keys, block_start, suffix_span, 1)
        values_blk = lax.dynamic_slice_in_dim(stored_values, block_start, suffix_span, 1)
        scores = (
            jnp.einsum("pbgqd,btgd->pbgqt", query_own, keys_blk, preferred_element_type=jnp.float32)
            * score_scale
        )
        position = block_start + jnp.arange(suffix_span, dtype=jnp.int32)
        visible = position[None, :] < lengths[:, None]
        scores = jnp.where(visible[None, :, None, None, :], scores, -jnp.inf)
        new_max = jnp.maximum(run_max, jnp.max(scores, axis=-1))
        rescale = jnp.exp(run_max - new_max)
        weights = jnp.exp(scores - new_max[..., None])
        run_total = run_total * rescale + jnp.sum(weights, axis=-1)
        run_sum = run_sum * rescale[..., None] + jnp.einsum(
            "pbgqt,btgd->pbgqd",
            weights.astype(jnp.bfloat16),
            values_blk,
            preferred_element_type=jnp.float32,
        )
        return (new_max, run_total, run_sum)

    own_max, own_total, own_sum = lax.fori_loop(
        0, block_limit, suffix_step, (own_max, own_total, own_sum)
    )
    out_grid = part_out.reshape(
        1, steps_count, n_prefix * n_replica, branch_local, heads_local, HEAD_SIZE
    )
    lse_grid = part_lse.reshape(1, steps_count, n_prefix * n_replica, branch_local, heads_local)
    got_out, got_lse = (
        lax.all_to_all(out_grid, ("prefix", "replica"), split_axis=2, concat_axis=0, tiled=True),
        lax.all_to_all(lse_grid, ("prefix", "replica"), split_axis=2, concat_axis=0, tiled=True),
    )
    stacked_out = got_out.reshape(
        n_prefix * n_replica, steps_count, branch_local, heads_local, HEAD_SIZE
    )
    stacked_lse = got_lse.reshape(n_prefix * n_replica, steps_count, branch_local, heads_local)
    own_max = own_max.reshape(steps_count, branch_local, heads_local)
    own_total = own_total.reshape(steps_count, branch_local, heads_local)
    own_sum = own_sum.reshape(steps_count, branch_local, heads_local, HEAD_SIZE)
    combined_max = jnp.maximum(own_max, jnp.max(stacked_lse, axis=0))
    own_factor = jnp.exp(own_max - combined_max)
    far_factor = jnp.exp(stacked_lse - combined_max)
    numer = own_sum * own_factor[..., None] + jnp.sum(far_factor[..., None] * stacked_out, axis=0)
    denom = own_total * own_factor + jnp.sum(far_factor, axis=0)
    attention = (
        (numer / denom[..., None])
        .astype(jnp.bfloat16)
        .reshape(steps_count, branch_local, row_width)
    )
    piece_rows = lax.all_gather(attention, ("prefix", "replica"), axis=1, tiled=True)
    flat_rows = piece_rows.reshape(-1, row_width)
    product = jnp.dot(flat_rows, out_weight, preferred_element_type=jnp.float32)
    terms = product.reshape(steps_count, piece_rows.shape[1], out_weight.shape[1])
    projected = lax.psum_scatter(
        terms.astype(jnp.bfloat16), "tensor", scatter_dimension=1, tiled=True
    )
    return projected


def solution(mesh):
    placed = (
        P(None, ("prefix", "replica"), "tensor"),
        P(("prefix", "replica"), "tensor"),
        P(("prefix", "replica"), "tensor"),
        P(("prefix", "replica"), None, "tensor"),
        P(("prefix", "replica"), None, "tensor"),
        P(None, ("prefix", "replica"), "tensor"),
        P(None, ("prefix", "replica"), "tensor"),
        P(("prefix", "replica")),
        P("tensor", ("prefix", "replica")),
    )
    return jax.shard_map(
        local,
        mesh=mesh,
        in_specs=placed,
        out_specs=P(None, "tensor", ("prefix", "replica")),
        check_vma=False,
    )
```

profile of v0, /device:TPU:1, one launch (start us, length us, event | category | flops | bytes accessed | tf_op | source)
XLA Modules:
  0.0 606.6 jit_solution(17341705171472981056)
XLA Ops:
  19.4 173.2 %all-gather.3.cloned.1.call-done = bf16[4,64,2048]{2,0,1:T(4,128)(2,1)} async-done(((bf16[4,1,2048]{2,0,1:T(4,128)(2,1)}), bf16[4,64,2048]{2,0,1:T(4,128)(2,1)}) %all-gather.3.cloned.1.call-update) | async-done | bytes 1048592 | tf_op jit(solution)/shard_map/all_gather | solution.py:31
  194.9 116.7 %while.30 = (s32[]{:T(128)}, f32[256,2,8]{0,2,1:T(8,128)S(1)}, f32[256,2,8]{0,2,1:T(8,128)}, f32[256,2,8,128]{0,3,2,1:T(8,128)S(1)}, bf16[6,512,2,128]{3,2,1,0:T...) while((s32[]{:T(128)}, f32[256,2,8]{0,2,1:T(8,128)S(1)}, ...), condition=%wide.region_9.10_spmd.clone, body=%wide.region_6.0_spmd.clone.sunk | while | flops 1092112384 | bytes 32899244 | solution.py:66
  197.0 4.5 bitcast_reduce_fusion.3
  201.5 4.8 fusion.70
  208.8 5.6 bitcast_add_fusion.5
  216.5 4.5 bitcast_reduce_fusion.3
  221.0 4.8 fusion.70
  228.2 5.6 bitcast_add_fusion.5
  235.9 4.5 bitcast_reduce_fusion.3
  240.4 4.8 fusion.70
  247.7 5.6 bitcast_add_fusion.5
  255.4 4.5 bitcast_reduce_fusion.3
  259.9 4.8 fusion.70
  267.1 5.6 bitcast_add_fusion.5
  279.3 4.8 fusion.70
  286.6 5.6 bitcast_add_fusion.5
  298.8 4.8 fusion.70
  306.0 5.6 bitcast_add_fusion.5
  314.1 13.5 %all-to-all-start = ((f32[1,4,64,1,16]{4,1,3,0,2:T(4,128)}), f32[1,4,64,1,16]{4,1,3,0,2:T(4,128)S(1)}, u32[]{:S(2)}, u32[]{:S(2)}) async-start(f32[1,4,64,1,16]{4,1,3,0,2:T(4,128)} %copy.84), calls=%async_computation | async-start | bytes 262144 | tf_op jit(solution)/shard_map/all_to_all | solution.py:131
  337.5 6.0 all-to-all-start.1
  343.6 4.7 while.29
  349.0 45.0 %all-to-all-done.1 = f32[1,4,64,1,16,128]{5,4,1,3,0,2:T(8,128)S(1)} async-done(((f32[1,4,64,1,16,128]{5,4,1,3,0,2:T(8,128)}), f32[1,4,64,1,16,128]{5,4,1,3,0,2:T(8,128)S(1)}, u32[]{:S(2)}, u32[]{:S(2)}) %all-to-all-start.1) | async-done | bytes 2097184 | tf_op jit(solution)/shard_map/all_to_all | solution.py:130
  395.4 176.6 %all-gather.5.cloned.1.call-done = bf16[4,64,2048]{2,0,1:T(4,128)(2,1)} async-done(((bf16[4,1,2048]{2,0,1:T(4,128)(2,1)}), bf16[4,64,2048]{2,0,1:T(4,128)(2,1)}) %all-gather.5.cloned.1.call-update) | async-done | bytes 1048592 | tf_op jit(solution)/shard_map/all_gather | solution.py:150
  575.2 24.9 %reduce-scatter.2.cloned.1.call-done = bf16[4,16,80]{2,1,0:T(8,128)(2,1)} async-done(((bf16[4,64,80]{2,1,0:T(8,128)(2,1)}), bf16[4,16,80]{2,1,0:T(8,128)(2,1)}) %reduce-scatter.2.cloned.1.call-update) | async-done | bytes 10256 | tf_op jit(solution)/shard_map/reduce_scatter | solution.py:154
  (140 shorter events, 73.0 us)
Async XLA Ops:
  6.5 565.5 %copy-start = (bf16[2048,80]{0,1:T(8,128)(2,1)S(1)}, bf16[2048,80]{0,1:T(8,128)(2,1)}, u32[]{:S(2)}) copy-start(bf16[2048,80]{0,1:T(8,128)(2,1)} %param.21) | copy-start | bytes 983044
  6.5 186.1 %all-gather.3.cloned.1.call-start = ((), (), s32[]{:S(2)}) async-start(), calls=%async_computation.3 | async-start | bytes 1064960 | tf_op jit(solution)/shard_map/all_gather | solution.py:31
  11.4 3.6 copy-start.8
  11.4 3.6 copy-start.5
  11.4 5.2 copy-start.6
  11.4 6.2 %copy-start.10 = (bf16[4,1,256]{2,0,1:T(4,128)(2,1)S(1)}, bf16[4,1,256]{2,0,1:T(4,128)(2,1)}, u32[]{:S(2)}) copy-start(bf16[4,1,256]{2,0,1:T(4,128)(2,1)} %param.18) | copy-start | bytes 6148
  201.5 4.8 copy-start.2
  221.0 4.8 copy-start.2
  225.8 0.6 copy-start.3
  240.4 4.8 copy-start.2
  259.9 4.8 copy-start.2
  264.7 0.6 copy-start.3
  279.3 4.8 copy-start.2
  284.1 0.6 copy-start.3
  298.8 4.8 copy-start.2
  303.6 0.6 copy-start.3
  314.1 23.4 %all-to-all-start = ((f32[1,4,64,1,16]{4,1,3,0,2:T(4,128)}), f32[1,4,64,1,16]{4,1,3,0,2:T(4,128)S(1)}, u32[]{:S(2)}, u32[]{:S(2)}) async-start(f32[1,4,64,1,16]{4,1,3,0,2:T(4,128)} %copy.84), calls=%async_computation | async-start | bytes 262144 | tf_op jit(solution)/shard_map/all_to_all | solution.py:131
  333.1 10.5 %copy-start.1 = (bf16[1,1024,256]{1,2,0:T(8,128)(2,1)S(1)}, bf16[1,1024,256]{1,2,0:T(8,128)(2,1)}, u32[]{:S(2)}) copy-start(bf16[1,1024,256]{1,2,0:T(8,128)(2,1)} %copy.75) | copy-start | bytes 1572868
  333.1 10.5 %copy-start.4 = (f32[4,1,2,8]{3,2,0,1:T(2,128)S(1)}, f32[4,1,2,8]{3,2,0,1:T(2,128)}, u32[]{:S(2)}) copy-start(f32[4,1,2,8]{3,2,0,1:T(2,128)} %get-tuple-element.369) | copy-start | bytes 772
  333.1 10.5 %copy-start.7 = (f32[4,1,2,8]{3,2,0,1:T(2,128)S(1)}, f32[4,1,2,8]{3,2,0,1:T(2,128)}, u32[]{:S(2)}) copy-start(f32[4,1,2,8]{3,2,0,1:T(2,128)} %get-tuple-element.370) | copy-start | bytes 772
  333.1 10.5 %copy-start.9 = (bf16[4,1,2,8,128]{4,3,0,2,1:T(8,128)(2,1)S(1)}, bf16[4,1,2,8,128]{4,3,0,2,1:T(8,128)(2,1)}, u32[]{:S(2)}) copy-start(bf16[4,1,2,8,128]{4,3,0,2,1:T(8,128)(2,1)} %copy.77) | copy-start | bytes 49156
  337.5 56.5 %all-to-all-start.1 = ((f32[1,4,64,1,16,128]{5,4,1,3,0,2:T(8,128)}), f32[1,4,64,1,16,128]{5,4,1,3,0,2:T(8,128)S(1)}, u32[]{:S(2)}, u32[]{:S(2)}) async-start(f32[1,4,64,1,16,128]{5,4,1,3,0,2:T(8,128)} %copy.87), calls=%async_computation.1 | async-start | bytes 4194304 | tf_op jit(solution)/shard_map/all_to_all | solution.py:130
  343.5 228.5 %all-gather.5.cloned.1.call-start = ((), (), s32[]{:S(2)}) async-start(), calls=%async_computation.4 | async-start | bytes 1064960 | tf_op jit(solution)/shard_map/all_gather | solution.py:150
  395.4 204.7 %reduce-scatter.2.cloned.1.call-start = ((), (), s32[]{:S(2)}) async-start(), calls=%async_computation.5 | async-start | bytes 81920 | tf_op jit(solution)/shard_map/reduce_scatter | solution.py:154
  (2 other events, 1.2 us)
Sparse Core Ops, SparseCore 0:
  9.2 183.3 all-gather.2
  395.5 176.5 all-gather.4
  575.3 24.7 reduce-scatter.1
where the time goes:
time: 609 us; the launch traced here: 607 us
  waiting for transfers between devices  425 us (70%)
  matrix products  67.4 us (11%)
  local copies, waits for them, and re-layouts  45.6 us (7%)
  other arithmetic  34.8 us (6%)
  starting transfers between devices  19.5 us (3%)
  between operations  14 us (2%)
    all_gather x1, waiting for transfers between devices, local(): lax.all_gather(attention, ('prefix', 'replica'), axis=1, tiled=True)  177 us
    all_gather x1, waiting for transfers between devices, local(): lax.all_gather(queries, ('prefix', 'replica'), axis=1, tiled=True)  173 us
    all_to_all x1, waiting for transfers between devices, local(): lax.all_to_all(out_grid, ('prefix', 'replica'), split_axis=2, concat_axis...  45 us
    dot_general x6, matrix products, prefix_step(): jnp.einsum('rgqk,kgd->rgqd', weights.astype(jnp.bfloat16), values_blk, pr...  33.5 us
    reduce_sum x6, other arithmetic, prefix_step(): run_total = run_total * rescale + jnp.sum(weights, axis=-1)  28.7 us
    dot_general x6, matrix products, prefix_step(): jnp.einsum('rgqd,kgd->rgqk', query_all, keys_blk, preferred_element_type=...  26.8 us
    reduce_scatter x1, waiting for transfers between devices, local(): lax.psum_scatter(terms.astype(jnp.bfloat16), 'tensor', scatter_dimension=...  24.9 us
    dynamic_slice x12, local copies, waits for them, and re-layouts, local(): lax.scan(prefix_step, initial_state, (blocked_keys, blocked_values))  23.7 us
  transfers between devices with their start and end apart: 5, of which 5 were waited for; matrix products, arithmetic and copies ran while one was open for 4% of the time, Pallas kernels for 0%

commit v1 on v0

v1 whole, which is shorter than its diff:
```python
import functools

import jax
import jax.numpy as jnp
from jax import lax
from jax.experimental import pallas as pl
from jax.experimental.pallas import tpu as pltpu
from jax.sharding import PartitionSpec as P

HEAD = 128
LOG2_SCALE = HEAD ** (-0.5) * 1.4426950408889634
NX, NZ = 4, 8
F32, BF16 = jnp.float32, jnp.bfloat16
PLANE = ("prefix", "replica")
VMEM = pl.BlockSpec(memory_space=pltpu.VMEM)
SMEM = pl.BlockSpec(memory_space=pltpu.SMEM)


def params(mib=8):
    return pltpu.CompilerParams(vmem_limit_bytes=mib << 20)


def plane_index(x, z, core):
    return ((z // 2) * 2 + core) * 8 + (z % 2) * 4 + x


ZC_GROUPS = [[plane_index(x, z, c) for z in range(NZ) for c in range(2)] for x in range(NX)]
CORE_SWAP = [(p, p ^ 1) for p in range(8)]


Z_PARTNERS = (
    [z ^ 1 for z in range(NZ)],
    [(z - 1) % NZ if z % 2 == 0 else (z + 1) % NZ for z in range(NZ)],
    [(z + 3) % NZ if z % 2 == 0 else (z - 3) % NZ for z in range(NZ)],
)


def z_exchange(step):
    return [
        (plane_index(x, z, c), plane_index(x, Z_PARTNERS[step][z], c))
        for x in range(NX)
        for z in range(NZ)
        for c in range(2)
    ]


def x_shift(k):
    return [(zl * 4 + x, zl * 4 + (x + k) % 4) for zl in range(2) for x in range(4)]


ROWS = NZ * 64
PACKED = (ROWS + 16, HEAD)


def eye():
    return lax.broadcasted_iota(jnp.int32, (HEAD, HEAD), 0) == lax.broadcasted_iota(
        jnp.int32, (HEAD, HEAD), 1
    )


def pack(o_ref, parts):
    rows = []
    for i, (out, lse) in enumerate(parts):
        o_ref[i * HEAD : (i + 1) * HEAD, :] = out.astype(BF16)
        rows.append(jnp.sum(jnp.where(eye(), lse, 0.0), axis=0, keepdims=True))
    rows = jnp.concatenate(rows, axis=0)
    high = rows.astype(BF16).astype(F32)
    middle = (rows - high).astype(BF16).astype(F32)
    low = rows - high - middle
    stats = jnp.concatenate([high, middle, low, jnp.zeros_like(low)], axis=0)
    o_ref[ROWS:, :] = stats.astype(BF16)


def unpack(ref):
    stats = ref[ROWS:, :].astype(F32)
    rows = stats[0:4] + stats[4:8] + stats[8:12]
    parts = []
    for i in range(4):
        lse = jnp.sum(jnp.where(eye(), rows[i : i + 1], 0.0), axis=1, keepdims=True)
        parts.append((ref[i * HEAD : (i + 1) * HEAD, :].astype(F32), lse))
    return parts


def merge(parts):
    top = functools.reduce(jnp.maximum, [lse for _, lse in parts])
    factors = [jnp.exp2(lse - top) for _, lse in parts]
    total = functools.reduce(jnp.add, factors)
    summed = functools.reduce(jnp.add, [f * out for f, (out, _) in zip(factors, parts)])
    return summed / total, top + jnp.log2(total)


def query_kernel(q_ref, o_ref, flat_ref):
    q = q_ref[...].astype(F32)
    rows = jnp.concatenate([q[:, i * HEAD : (i + 1) * HEAD] for i in range(16)], axis=0)
    rows = rows.astype(BF16)
    flat_ref[...] = rows
    for z in range(NZ):
        o_ref[z] = rows


def arrange_kernel(core_ref, k_ref, v_ref, send_ref, sems):
    columns = pl.ds(pl.multiple_of((1 - core_ref[0]) * HEAD, HEAD), HEAD)
    copies = [
        pltpu.make_async_copy(
            ref.at[:, columns], send_ref.at[:, pl.ds(i * HEAD, HEAD)], sems.at[i]
        )
        for i, ref in enumerate((k_ref, v_ref))
    ]
    for copy in copies:
        copy.start()
    for copy in copies:
        copy.wait()


def suffix_kernel(length_ref, core_ref, q_ref, k_ref, v_ref, nk_ref, nv_ref, own_ref, send_ref):
    length = length_ref[0]
    slots = k_ref.shape[0]
    visible = lax.broadcasted_iota(jnp.int32, (32, slots), 1) < length
    new_row = lax.broadcasted_iota(jnp.int32, (32, 16), 0) % 4
    new_col = lax.broadcasted_iota(jnp.int32, (32, 16), 1)
    causal = new_col <= new_row
    nt = (((1,), (1,)), ((), ()))
    empty = jnp.zeros((12, 2 * HEAD), F32)
    new_keys = jnp.concatenate([nk_ref[...].astype(F32), empty], axis=0).astype(BF16)
    new_values = jnp.concatenate([nv_ref[...].astype(F32), empty], axis=0).astype(BF16)
    results = []
    for g in range(2):
        columns = slice(g * HEAD, (g + 1) * HEAD)
        q = q_ref[g * 32 : (g + 1) * 32, :]
        s = lax.dot_general(q, k_ref[:, columns], nt, preferred_element_type=F32)
        t = lax.dot_general(q, new_keys[:, columns], nt, preferred_element_type=F32)
        s = jnp.where(visible, s * LOG2_SCALE, -jnp.inf)
        t = jnp.where(causal, t * LOG2_SCALE, -jnp.inf)
        top = jnp.maximum(
            jnp.max(s, axis=1, keepdims=True), jnp.max(t, axis=1, keepdims=True)
        )
        ws, wt = jnp.exp2(s - top), jnp.exp2(t - top)
        total = jnp.sum(ws, axis=1, keepdims=True) + jnp.sum(wt, axis=1, keepdims=True)
        summed = jnp.dot(ws.astype(BF16), v_ref[:, columns], preferred_element_type=F32)
        summed += jnp.dot(wt.astype(BF16), new_values[:, columns], preferred_element_type=F32)
        lse = jnp.broadcast_to(top + jnp.log2(total), (32, HEAD))
        results.append(jnp.concatenate([summed / total, lse], axis=0))
    first = core_ref[0] == 0
    own_ref[...] = jnp.where(first, results[0], results[1])
    send_ref[...] = jnp.where(first, results[1], results[0])


def fetch_kernel(away_ref, o_ref, sem):
    copy = pltpu.make_async_copy(away_ref, o_ref, sem)
    copy.start()
    copy.wait()


def attend_kernel(span, core_ref, q_ref, k_ref, v_ref, other_ref, o_ref):
    q = q_ref[...].reshape(NZ * 64, HEAD)
    top = summed = None
    mine = pl.ds(pl.multiple_of(core_ref[0] * HEAD, HEAD), HEAD)
    ones = jnp.ones((span, HEAD), BF16)
    sources = ((k_ref, mine, v_ref, mine), (other_ref, pl.ds(0, HEAD), other_ref, pl.ds(HEAD, HEAD)))
    for keys, key_columns, values, value_columns in sources:
        for start in range(0, keys.shape[0], span):
            rows = pl.ds(start, span)
            s = lax.dot_general(
                q,
                keys[rows, key_columns],
                (((1,), (1,)), ((), ())),
                preferred_element_type=F32,
            )
            here = jnp.max(s, axis=1, keepdims=True)
            new_top = here if top is None else jnp.maximum(top, here)
            w = jnp.exp2((s - new_top) * LOG2_SCALE).astype(BF16)
            widened = jnp.concatenate([values[rows, value_columns], ones], axis=1)
            part = jnp.dot(w, widened, preferred_element_type=F32)
            if top is None:
                summed = part
            else:
                summed = summed * jnp.exp2((top - new_top) * LOG2_SCALE) + part
            top = new_top
    total = summed[:, HEAD:]
    out = summed[:, :HEAD] / total
    lse = top * LOG2_SCALE + jnp.log2(total)
    blocks = [slice(i * HEAD, (i + 1) * HEAD) for i in range(4)]
    pack(o_ref, [(out[rows], lse[rows]) for rows in blocks])


def merge_kernel(z_ref, core_ref, a_ref, b_ref, c_ref, d_ref, own_ref, sibling_ref, o_ref):
    own, sibling = own_ref[...], sibling_ref[...]
    first = core_ref[0] == 0
    low, high = jnp.where(first, own, sibling), jnp.where(first, sibling, own)
    near_out = jnp.concatenate([low[0:32], high[0:32]] * 2, axis=0)
    near_lse = jnp.concatenate([low[32:], high[32:]] * 2, axis=0)
    half = lax.broadcasted_iota(jnp.int32, (HEAD, HEAD), 0) // 64
    far = [unpack(ref) for ref in (a_ref, b_ref, c_ref, d_ref)]
    merged = []
    for i in range(4):
        here = jnp.where(half + 2 * i == z_ref[0], near_lse, -jnp.inf)[:, 0:1]
        merged.append(merge([part[i] for part in far] + [(near_out, here)]))
    pack(o_ref, merged)


def pair_kernel(a_ref, b_ref, o_ref):
    pack(o_ref, [merge(list(parts)) for parts in zip(unpack(a_ref), unpack(b_ref))])


def finish_kernel(a_ref, b_ref, o_ref):
    rows = []
    for parts in zip(unpack(a_ref), unpack(b_ref)):
        out, _ = merge(list(parts))
        for start in (0, 64):
            heads = [
                jnp.concatenate(
                    [
                        out[start + h * 4 : start + h * 4 + 4],
                        out[start + 32 + h * 4 : start + 36 + h * 4],
                    ],
                    axis=0,
                )
                for h in range(8)
            ]
            rows.append(jnp.concatenate(heads, axis=1))
    o_ref[...] = jnp.concatenate(rows, axis=0).astype(BF16)


def project_kernel(x_ref, core_ref, a_ref, b_ref, c_ref, d_ref, w_ref, ws_ref, own_ref, send_ref):
    nt = (((1,), (1,)), ((), ()))
    width = ws_ref.shape[1]
    mine = w_ref[:, pl.ds(pl.multiple_of(core_ref[0] * width, width), width)]
    other = ws_ref[...]
    for k, ref in enumerate((a_ref, b_ref, c_ref, d_ref)):
        place = lax.rem(x_ref[0] + k, NX)
        rows = ref[...]
        for weight, o_ref in ((mine, own_ref), (other, send_ref)):
            product = lax.dot_general(rows, weight, nt, preferred_element_type=F32)
            product = product.astype(BF16)
            for t in range(4):
                o_ref[t, place] = product[t * 16 : (t + 1) * 16]


def halve_kernel(t_ref, a_ref, b_ref, keep_ref, send_ref):
    t = t_ref[0]
    partner = t + 1 - 2 * lax.rem(t, 2)
    for ref, owner in ((keep_ref, t), (send_ref, partner)):
        for i, block in enumerate((owner, 3 - owner)):
            ref[i] = (a_ref[block].astype(F32) + b_ref[block].astype(F32)).astype(BF16)


def quarter_kernel(a_ref, b_ref, keep_ref, send_ref):
    keep_ref[...] = a_ref[0].astype(F32) + b_ref[0].astype(F32)
    send_ref[...] = (a_ref[1].astype(F32) + b_ref[1].astype(F32)).astype(BF16)


def sum_kernel(a_ref, b_ref, o_ref):
    total = (a_ref[...] + b_ref[...].astype(F32)).reshape(64, a_ref.shape[2])
    row = lax.broadcasted_iota(jnp.int32, (64, 64), 0)
    column = lax.broadcasted_iota(jnp.int32, (64, 64), 1)
    source = (row % 4) * 16 + ((row // 4) % 2) * 8 + ((row // 8) % 2) * 4 + row // 16
    moved = jnp.dot(
        (column == source).astype(BF16), total.astype(BF16), preferred_element_type=F32
    ).astype(BF16)
    for p in range(4):
        o_ref[p] = moved[p * 16 : (p + 1) * 16]


def call(kernel, shapes, specs, name, flops=0, moved=0, exps=0, mib=8, scratch=()):
    return pl.pallas_call(
        kernel,
        out_shape=shapes,
        in_specs=specs,
        out_specs=jax.tree.map(lambda _: VMEM, shapes),
        scratch_shapes=scratch,
        compiler_params=params(mib),
        cost_estimate=pl.CostEstimate(flops=flops, bytes_accessed=moved, transcendentals=exps),
        name=name,
    )


def shape(dims, dtype=BF16):
    return jax.ShapeDtypeStruct(dims, dtype)


def local(
    queries,
    common_prefix_keys,
    common_prefix_values,
    branch_suffix_keys,
    branch_suffix_values,
    position_keys,
    position_values,
    lengths,
    out_weight,
):
    core = lax.rem(lax.axis_index("prefix"), 2).reshape(1)
    x = lax.rem(lax.axis_index("replica"), NX).reshape(1)
    z = (lax.axis_index("prefix") // 2 * 2 + lax.axis_index("replica") // NX).reshape(1)
    tensor = lax.axis_index("tensor").reshape(1)
    kv_rows = common_prefix_keys.shape[0]
    slots = branch_suffix_keys.shape[1]

    query_rows, query_flat = call(
        query_kernel, [shape((NZ, 64, HEAD)), shape((64, HEAD))], [VMEM], "query"
    )(queries.reshape(4, 2048))
    near_queries = lax.all_to_all(
        query_rows.reshape(2 * NZ, 32, HEAD),
        PLANE,
        0,
        0,
        tiled=True,
        axis_index_groups=ZC_GROUPS,
    ).reshape(NZ, 64, HEAD)

    send = pl.pallas_call(
        arrange_kernel,
        out_shape=shape((kv_rows, 2 * HEAD)),
        in_specs=[SMEM] + [pl.BlockSpec(memory_space=pltpu.HBM)] * 2,
        out_specs=pl.BlockSpec(memory_space=pltpu.HBM),
        scratch_shapes=[pltpu.SemaphoreType.DMA((2,))],
        compiler_params=params(),
        cost_estimate=pl.CostEstimate(
            flops=0, bytes_accessed=kv_rows * HEAD * 8, transcendentals=0
        ),
        name="arrange",
    )(core, common_prefix_keys, common_prefix_values)
    near_queries, send = lax.optimization_barrier((near_queries, send))
    other = call(
        fetch_kernel,
        shape((kv_rows, 2 * HEAD)),
        [pl.BlockSpec(memory_space=pl.ANY)],
        "fetch",
        moved=kv_rows * HEAD * 4,
        scratch=[pltpu.SemaphoreType.DMA],
    )(lax.ppermute(send, "prefix", CORE_SWAP))

    weight = out_weight.T
    width = weight.shape[1] // 2
    weight_send = lax.dynamic_slice_in_dim(weight, (1 - core[0]) * width, width, 1)
    weight_other = lax.ppermute(weight_send, "prefix", CORE_SWAP)

    own, own_send = call(
        suffix_kernel,
        [shape((64, HEAD), F32)] * 2,
        [SMEM] * 2 + [VMEM] * 5,
        "suffix",
        flops=2 * 32 * slots * HEAD * 4,
        moved=slots * HEAD * 8,
        exps=64 * slots,
    )(
        lengths,
        core,
        query_flat,
        branch_suffix_keys[0],
        branch_suffix_values[0],
        position_keys.reshape(4, 2 * HEAD),
        position_values.reshape(4, 2 * HEAD),
    )
    sibling = lax.ppermute(own_send, "prefix", CORE_SWAP)

    attend = call(
        functools.partial(attend_kernel, 512),
        shape(PACKED),
        [SMEM] + [VMEM] * 4,
        "attend",
        flops=4 * 512 * 2 * kv_rows * HEAD,
        moved=kv_rows * HEAD * 12,
        exps=512 * 2 * kv_rows,
        mib=16,
    )
    chunk_queries = [near_queries] + [
        lax.ppermute(near_queries, "replica", x_shift(-k)) for k in (1, 2, 3)
    ]
    partial = [
        attend(core, q, common_prefix_keys, common_prefix_values, other) for q in chunk_queries
    ]
    back = [lax.ppermute(partial[k], "replica", x_shift(k)) for k in (1, 2, 3)]
    merged = call(
        merge_kernel, shape(PACKED), [SMEM] * 2 + [VMEM] * 6, "merge", moved=6 * 135168
    )(z, core, partial[0], *back, own, sibling)
    for step in (0, 1):
        arrived = lax.ppermute(merged, PLANE, z_exchange(step))
        merged = call(pair_kernel, shape(PACKED), [VMEM] * 2, "pair")(merged, arrived)
    arrived = lax.ppermute(merged, PLANE, z_exchange(2))
    near_rows = call(finish_kernel, shape((64, 1024)), [VMEM] * 2, "finish")(merged, arrived)
    chunk_rows = [near_rows] + [
        lax.ppermute(near_rows, "replica", x_shift(-k)) for k in (1, 2, 3)
    ]
    columns = out_weight.shape[1]
    block = (NX, 16, columns)
    product, product_send = call(
        project_kernel,
        [shape((4,) + block)] * 2,
        [SMEM] * 2 + [VMEM] * 6,
        "project",
        flops=2 * 256 * 1024 * 160,
        moved=1 << 20,
    )(x, core, *chunk_rows, weight, weight_other)
    product_other = lax.ppermute(product_send, "prefix", CORE_SWAP)
    kept, sent = call(
        halve_kernel, [shape((2,) + block)] * 2, [SMEM] + [VMEM] * 2, "halve"
    )(tensor, product, product_other)
    arrived = lax.ppermute(sent, "tensor", [(t, t ^ 1) for t in range(4)])
    kept, sent = call(
        quarter_kernel, [shape(block, F32), shape(block)], [VMEM] * 2, "quarter"
    )(kept, arrived)
    arrived = lax.ppermute(sent, "tensor", [(t, 3 - t) for t in range(4)])
    return call(sum_kernel, shape((4, 16, columns)), [VMEM] * 2, "sum")(kept, arrived)


def solution(mesh):
    placed = (
        P(None, ("prefix", "replica"), "tensor"),
        P(("prefix", "replica"), "tensor"),
        P(("prefix", "replica"), "tensor"),
        P(("prefix", "replica"), None, "tensor"),
        P(("prefix", "replica"), None, "tensor"),
        P(None, ("prefix", "replica"), "tensor"),
        P(None, ("prefix", "replica"), "tensor"),
        P(("prefix", "replica")),
        P("tensor", ("prefix", "replica")),
    )
    return jax.shard_map(
        local,
        mesh=mesh,
        in_specs=placed,
        out_specs=P(None, "tensor", ("prefix", "replica")),
        check_vma=False,
    )
```

time: 609 us -> 94.1 us (0.15)
  waiting for transfers between devices: 425 us -> 25.3 us
  matrix products: 67.4 us -> 0 us
  local copies, waits for them, and re-layouts: 45.6 us -> 6.24 us
  other arithmetic: 34.8 us -> 0 us
  Pallas kernels: 0 us -> 22.2 us
  starting transfers between devices: 19.5 us -> 38.2 us
  between operations: 14 us -> 0.82 us
    all_gather x2 -> x0, waiting for transfers between devices: 350 us -> none  [the longest x1 177 us: local(): lax.all_gather(attention, ('prefix', 'replica'), axis=1, tiled=True)]
    dot_general x19 -> x0, matrix products: 67.4 us -> none  [the longest x6 33.5 us: prefix_step(): jnp.einsum('rgqk,kgd->rgqd', weights.astype(jnp.bfloat16), values_blk, pr...]
    all_to_all x2 -> x1, waiting for transfers between devices: 49.5 us -> 6.05 us  [local(): lax.all_to_all(query_rows.reshape(2 * NZ, 32, HEAD), PLANE, 0, 0, tiled=T...]
    reduce_sum x11 -> x0, other arithmetic: 29.8 us -> none  [the longest x6 28.7 us: prefix_step(): run_total = run_total * rescale + jnp.sum(weights, axis=-1)]
    ppermute x0 -> x18, starting transfers between devices: none -> 28.2 us  [the longest x1 8.14 us: local(): product_other = lax.ppermute(product_send, 'prefix', CORE_SWAP)]
    reduce_scatter x1 -> x0, waiting for transfers between devices: 24.9 us -> none  [local(): lax.psum_scatter(terms.astype(jnp.bfloat16), 'tensor', scatter_dimension=...]
    dynamic_slice x12 -> x1, local copies, waits for them, and re-layouts: 23.7 us -> 0.01 us  [local(): lax.dynamic_slice_in_dim(weight, (1 - core[0]) * width, width, 1)]
    pallas_call x0 -> x16, Pallas kernels: none -> 22.2 us  [the longest x4 17.2 us: local(): attend(core, q, common_prefix_keys, common_prefix_values, other)]
  transfers between devices with their start and end apart: 5 -> 19, of which waited for: 5 -> 10; matrix products, arithmetic and copies ran while one was open for 4% -> 0% of each run, Pallas kernels for 0% -> 20%
where the time goes in v1:
time: 94.1 us; the launch traced here: 92.7 us
  starting transfers between devices  38.2 us (41%)
  waiting for transfers between devices  25.3 us (27%)
  Pallas kernels  22.2 us (24%)
  local copies, waits for them, and re-layouts  6.24 us (7%)
    pallas_call x4, Pallas kernels, local(): attend(core, q, common_prefix_keys, common_prefix_values, other)  17.2 us
    all_to_all x1, starting transfers between devices, local(): lax.all_to_all(query_rows.reshape(2 * NZ, 32, HEAD), PLANE, 0, 0, tiled=T...  9.98 us
    ppermute x2, waiting for transfers between devices, local(): arrived = lax.ppermute(merged, PLANE, z_exchange(step))  8.84 us
    ppermute x1, starting transfers between devices, local(): product_other = lax.ppermute(product_send, 'prefix', CORE_SWAP)  8.14 us
    unnamed x20, local copies, waits for them, and re-layouts  6.23 us
    all_to_all x1, waiting for transfers between devices, local(): lax.all_to_all(query_rows.reshape(2 * NZ, 32, HEAD), PLANE, 0, 0, tiled=T...  6.05 us
    ppermute x3, waiting for transfers between devices, local(): lax.ppermute(near_rows, 'replica', x_shift(-k))  5.02 us
    ppermute x3, starting transfers between devices, local(): back = [lax.ppermute(partial[k], 'replica', x_shift(k)) for k in (1, 2, 3)]  3.99 us
  transfers between devices with their start and end apart: 19, of which 10 were waited for; matrix products, arithmetic and copies ran while one was open for 0% of the time, Pallas kernels for 20%

profile of v1, /device:TPU:1, one launch (start us, length us, event | category | flops | bytes accessed | tf_op | source)
XLA Modules:
  0.0 92.7 jit_solution(3792333956819650501)
XLA Ops:
  1.4 10.0 %all-to-all-start = ((bf16[16,32,128]{2,1,0:T(8,128)(2,1)}), bf16[16,32,128]{2,1,0:T(8,128)(2,1)S(1)}, u32[]{:S(2)}, u32[]{:S(2)}) async-start(bf16[16,32,128]{2,1,0:T(8,128)(2,1)} %bitcast.5), calls=%async_computation | async-start | bytes 262144 | tf_op jit(solution)/shard_map/all_to_all | solution.py:302
  11.4 1.4 %copy-done = bf16[3072,256]{1,0:T(8,128)(2,1)S(1)} copy-done((bf16[3072,256]{1,0:T(8,128)(2,1)S(1)}, bf16[3072,256]{1,0:T(8,128)(2,1)}, u32[]{:S(2)}) %copy-start) | copy-done | bytes 1572888
  12.8 1.4 %copy-done.2 = bf16[3072,256]{1,0:T(8,128)(2,1)S(1)} copy-done((bf16[3072,256]{1,0:T(8,128)(2,1)S(1)}, bf16[3072,256]{1,0:T(8,128)(2,1)}, u32[]{:S(2)}) %copy-start.2) | copy-done | bytes 1572888
  14.5 6.0 %all-to-all-done = bf16[16,32,128]{2,1,0:T(8,128)(2,1)S(1)} async-done(((bf16[16,32,128]{2,1,0:T(8,128)(2,1)}), bf16[16,32,128]{2,1,0:T(8,128)(2,1)S(1)}, u32[]{:S(2)}, u32[]{:S(2)}) %all-to-all-start) | async-done | bytes 131104 | tf_op jit(solution)/shard_map/all_to_all | solution.py:302
  20.5 2.5 %collective-permute-start.1 = (bf16[8,64,128]{2,1,0:T(8,128)(2,1)S(1)}, bf16[8,64,128]{2,1,0:T(8,128)(2,1)S(1)}, u32[]{:S(2)}, u32[]{:S(2)}) collective-permute-start(bf16[8,64,128]{2,1,0:T(8,128)(2,1)S(1)} %bitcast.17), channel_id=1, source_target_pairs={{0,12},{4,0},{8,4},{12,8},{16,28},{20,16},{24,20},{28,24},{1,13},{... | collective-permute-start | bytes 393224 | tf_op jit(solution)/shard_map/ppermute | solution.py:368
  29.3 4.2 %attend.5 = bf16[528,128]{1,0:T(8,128)(2,1)S(1)} custom-call(s32[1]{0:T(128)} %bitcast.2.core_ref, bf16[8,64,128]{2,1,0:T(8,128)(2,1)S(1)} %collective-permute-done.1.q_ref, bf16[3072,256]{1,0:T(8,128)(2,1)S(1)} %copy-done.1, bf16[3072,256]{1,0:T(8,128)(2,1)S(1)} %copy-done.3, bf16[3072,256]{1,0:T(8,128)(2,1)S(1)} %fetch.1.other_ref), custom_call_target="tpu_custom_call" | custom-call | flops 1610612736 | bytes 4718592 | tf_op jit(solution)/shard_map/attend/pallas_call | solution.py:371
  33.5 1.2 %collective-permute-start.2 = (bf16[528,128]{1,0:T(8,128)(2,1)S(1)}, bf16[528,128]{1,0:T(8,128)(2,1)S(1)}, u32[]{:S(2)}, u32[]{:S(2)}) collective-permute-start(bf16[528,128]{1,0:T(8,128)(2,1)S(1)} %attend.5), channel_id=1, source_target_pairs={{0,4},{4,8},{8,12},{12,0},{16,20},{20,24},{24,28},{28,16},{1,5},{5... | collective-permute-start | bytes 405512 | tf_op jit(solution)/shard_map/ppermute | solution.py:373
  34.7 4.4 %attend.6 = bf16[528,128]{1,0:T(8,128)(2,1)S(1)} custom-call(s32[1]{0:T(128)} %bitcast.2.core_ref, bf16[8,64,128]{2,1,0:T(8,128)(2,1)S(1)} %collective-permute-done.3.q_ref, bf16[3072,256]{1,0:T(8,128)(2,1)S(1)} %copy-done.1, bf16[3072,256]{1,0:T(8,128)(2,1)S(1)} %copy-done.3, bf16[3072,256]{1,0:T(8,128)(2,1)S(1)} %fetch.1.other_ref), custom_call_target="tpu_custom_call" | custom-call | flops 1610612736 | bytes 4718592 | tf_op jit(solution)/shard_map/attend/pallas_call | solution.py:371
  39.1 1.8 %collective-permute-start.4 = (bf16[528,128]{1,0:T(8,128)(2,1)S(1)}, bf16[528,128]{1,0:T(8,128)(2,1)S(1)}, u32[]{:S(2)}, u32[]{:S(2)}) collective-permute-start(bf16[528,128]{1,0:T(8,128)(2,1)S(1)} %attend.6), channel_id=1, source_target_pairs={{0,8},{4,12},{8,0},{12,4},{16,24},{20,28},{24,16},{28,20},{1,9},{5... | collective-permute-start | bytes 405512 | tf_op jit(solution)/shard_map/ppermute | solution.py:373
  40.9 4.4 %attend.7 = bf16[528,128]{1,0:T(8,128)(2,1)S(1)} custom-call(s32[1]{0:T(128)} %bitcast.2.core_ref, bf16[8,64,128]{2,1,0:T(8,128)(2,1)S(1)} %collective-permute-done.5.q_ref, bf16[3072,256]{1,0:T(8,128)(2,1)S(1)} %copy-done.1, bf16[3072,256]{1,0:T(8,128)(2,1)S(1)} %copy-done.3, bf16[3072,256]{1,0:T(8,128)(2,1)S(1)} %fetch.1.other_ref), custom_call_target="tpu_custom_call" | custom-call | flops 1610612736 | bytes 4718592 | tf_op jit(solution)/shard_map/attend/pallas_call | solution.py:371
  46.2 4.2 %attend.4.a_ref = bf16[528,128]{1,0:T(8,128)(2,1)S(1)} custom-call(s32[1]{0:T(128)} %bitcast.2.core_ref, bf16[8,64,128]{2,1,0:T(8,128)(2,1)S(1)} %bitcast.20, bf16[3072,256]{1,0:T(8,128)(2,1)S(1)} %copy-done.1, bf16[3072,256]{1,0:T(8,128)(2,1)S(1)} %copy-done.3, bf16[3072,256]{1,0:T(8,128)(2,1)S(1)} %fetch.1.other_ref), custom_call_target="tpu_custom_call" | custom-call | flops 1610612736 | bytes 4718592 | tf_op jit(solution)/shard_map/attend/pallas_call | solution.py:371
  51.7 3.8 %collective-permute-done.8.b_ref = bf16[528,128]{1,0:T(8,128)(2,1)S(1)} collective-permute-done((bf16[528,128]{1,0:T(8,128)(2,1)S(1)}, bf16[528,128]{1,0:T(8,128)(2,1)S(1)}, u32[]{:S(2)}, u32[]{:S(2)}) %collective-permute-start.8) | collective-permute-done | bytes 135200 | tf_op jit(solution)/shard_map/ppermute | solution.py:378
  55.9 5.1 %collective-permute-done.9.b_ref = bf16[528,128]{1,0:T(8,128)(2,1)S(1)} collective-permute-done((bf16[528,128]{1,0:T(8,128)(2,1)S(1)}, bf16[528,128]{1,0:T(8,128)(2,1)S(1)}, u32[]{:S(2)}, u32[]{:S(2)}) %collective-permute-start.9) | collective-permute-done | bytes 135200 | tf_op jit(solution)/shard_map/ppermute | solution.py:378
  61.7 4.0 %collective-permute-start.14 = (bf16[80,1024]{1,0:T(8,128)(2,1)S(1)}, bf16[80,1024]{1,0:T(8,128)(2,1)S(1)}, u32[]{:S(2)}, u32[]{:S(2)}) collective-permute-start(bf16[80,1024]{1,0:T(8,128)(2,1)S(1)} %dynamic-slice_bitcast_fusion), channel_id=1, source_target_pairs={{0,32},{32,0},{64,96},{96,64},{128,160},{160,128},{192,224},{224,1... | collective-permute-start | bytes 491528 | tf_op jit(solution)/shard_map/ppermute | solution.py:336
  65.7 1.9 %collective-permute-done.10.b_ref = bf16[528,128]{1,0:T(8,128)(2,1)S(1)} collective-permute-done((bf16[528,128]{1,0:T(8,128)(2,1)S(1)}, bf16[528,128]{1,0:T(8,128)(2,1)S(1)}, u32[]{:S(2)}, u32[]{:S(2)}) %collective-permute-start.10) | collective-permute-done | bytes 135200 | tf_op jit(solution)/shard_map/ppermute | solution.py:380
  68.7 1.8 %collective-permute-start.12 = (bf16[64,1024]{1,0:T(8,128)(2,1)S(1)}, bf16[64,1024]{1,0:T(8,128)(2,1)S(1)}, u32[]{:S(2)}, u32[]{:S(2)}) collective-permute-start(bf16[64,1024]{1,0:T(8,128)(2,1)S(1)} %finish.1.a_ref), channel_id=1, source_target_pairs={{0,8},{4,12},{8,0},{12,4},{16,24},{20,28},{24,16},{28,20},{1,9},{5... | collective-permute-start | bytes 393224 | tf_op jit(solution)/shard_map/ppermute | solution.py:383
  70.5 1.3 %collective-permute-done.11.b_ref = bf16[64,1024]{1,0:T(8,128)(2,1)S(1)} collective-permute-done((bf16[64,1024]{1,0:T(8,128)(2,1)S(1)}, bf16[64,1024]{1,0:T(8,128)(2,1)S(1)}, u32[]{:S(2)}, u32[]{:S(2)}) %collective-permute-start.11) | collective-permute-done | bytes 131104 | tf_op jit(solution)/shard_map/ppermute | solution.py:383
  71.8 2.2 %collective-permute-done.12.c_ref = bf16[64,1024]{1,0:T(8,128)(2,1)S(1)} collective-permute-done((bf16[64,1024]{1,0:T(8,128)(2,1)S(1)}, bf16[64,1024]{1,0:T(8,128)(2,1)S(1)}, u32[]{:S(2)}, u32[]{:S(2)}) %collective-permute-start.12) | collective-permute-done | bytes 131104 | tf_op jit(solution)/shard_map/ppermute | solution.py:383
  74.0 1.5 %collective-permute-done.13.d_ref = bf16[64,1024]{1,0:T(8,128)(2,1)S(1)} collective-permute-done((bf16[64,1024]{1,0:T(8,128)(2,1)S(1)}, bf16[64,1024]{1,0:T(8,128)(2,1)S(1)}, u32[]{:S(2)}, u32[]{:S(2)}) %collective-permute-start.13) | collective-permute-done | bytes 131104 | tf_op jit(solution)/shard_map/ppermute | solution.py:383
  76.0 8.1 %collective-permute-start.15 = (bf16[4,4,16,80]{3,2,1,0:T(8,128)(2,1)S(1)}, bf16[4,4,16,80]{3,2,1,0:T(8,128)(2,1)S(1)}, u32[]{:S(2)}, u32[]{:S(2)}) collective-permute-start(bf16[4,4,16,80]{3,2,1,0:T(8,128)(2,1)S(1)} %get-tuple-element.24), channel_id=1, source_target_pairs={{0,32},{32,0},{64,96},{96,64},{128,160},{160,128},{192,224},{224,1... | collective-permute-start | bytes 122888 | tf_op jit(solution)/shard_map/ppermute | solution.py:395
  85.1 1.4 %collective-permute-start.16 = (bf16[2,4,16,80]{3,2,1,0:T(8,128)(2,1)S(1)}, bf16[2,4,16,80]{3,2,1,0:T(8,128)(2,1)S(1)}, u32[]{:S(2)}, u32[]{:S(2)}) collective-permute-start(bf16[2,4,16,80]{3,2,1,0:T(8,128)(2,1)S(1)} %get-tuple-element.26), channel_id=1, source_target_pairs={{0,1},{1,0},{2,3},{3,2},{4,5},{5,4},{6,7},{7,6},{8,9},{9,8},{10,11... | collective-permute-start | bytes 61448 | tf_op jit(solution)/shard_map/ppermute | solution.py:399
  86.5 1.5 %collective-permute-done.16.b_ref = bf16[2,4,16,80]{3,2,1,0:T(8,128)(2,1)S(1)} collective-permute-done((bf16[2,4,16,80]{3,2,1,0:T(8,128)(2,1)S(1)}, bf16[2,4,16,80]{3,2,1,0:T(8,128)(2,1)S(1)}, u32[]{:S(2)}, u32[]{:S(2)}) %collective-permute-start.16) | collective-permute-done | bytes 20512 | tf_op jit(solution)/shard_map/ppermute | solution.py:399
  87.9 2.8 %collective-permute-start.17 = (bf16[4,16,80]{2,1,0:T(8,128)(2,1)S(1)}, bf16[4,16,80]{2,1,0:T(8,128)(2,1)S(1)}, u32[]{:S(2)}, u32[]{:S(2)}) collective-permute-start(bf16[4,16,80]{2,1,0:T(8,128)(2,1)S(1)} %get-tuple-element.28), channel_id=1, source_target_pairs={{0,3},{1,2},{2,1},{3,0},{4,7},{5,6},{6,5},{7,4},{8,11},{9,10},{10,... | collective-permute-start | bytes 30728 | tf_op jit(solution)/shard_map/ppermute | solution.py:403
  90.8 1.1 %collective-permute-done.17.b_ref = bf16[4,16,80]{2,1,0:T(8,128)(2,1)S(1)} collective-permute-done((bf16[4,16,80]{2,1,0:T(8,128)(2,1)S(1)}, bf16[4,16,80]{2,1,0:T(8,128)(2,1)S(1)}, u32[]{:S(2)}, u32[]{:S(2)}) %collective-permute-start.17) | collective-permute-done | bytes 10272 | tf_op jit(solution)/shard_map/ppermute | solution.py:403
  (51 shorter events, 13.9 us)
Async XLA Ops:
  1.4 19.1 %all-to-all-start = ((bf16[16,32,128]{2,1,0:T(8,128)(2,1)}), bf16[16,32,128]{2,1,0:T(8,128)(2,1)S(1)}, u32[]{:S(2)}, u32[]{:S(2)}) async-start(bf16[16,32,128]{2,1,0:T(8,128)(2,1)} %bitcast.5), calls=%async_computation | async-start | bytes 262144 | tf_op jit(solution)/shard_map/all_to_all | solution.py:302
  11.4 1.4 %copy-start = (bf16[3072,256]{1,0:T(8,128)(2,1)S(1)}, bf16[3072,256]{1,0:T(8,128)(2,1)}, u32[]{:S(2)}) copy-start(bf16[3072,256]{1,0:T(8,128)(2,1)} %k_ref.9) | copy-start | bytes 4718596
  14.2 9.5 %copy-start.8 = (bf16[4,1,256]{2,0,1:T(4,128)(2,1)S(1)}, bf16[4,1,256]{2,0,1:T(4,128)(2,1)}, u32[]{:S(2)}) copy-start(bf16[4,1,256]{2,0,1:T(4,128)(2,1)} %param.14) | copy-start | bytes 6148
  14.2 9.5 %copy-start.9 = (bf16[4,1,256]{2,0,1:T(4,128)(2,1)S(1)}, bf16[4,1,256]{2,0,1:T(4,128)(2,1)}, u32[]{:S(2)}) copy-start(bf16[4,1,256]{2,0,1:T(4,128)(2,1)} %param.15) | copy-start | bytes 6148
  20.5 8.0 %collective-permute-start = (bf16[3072,256]{1,0:T(8,128)(2,1)S(1)}, bf16[3072,256]{1,0:T(8,128)(2,1)S(1)}, u32[]{:S(2)}, u32[]{:S(2)}) collective-permute-start(bf16[3072,256]{1,0:T(8,128)(2,1)S(1)} %arrange.1), channel_id=1, source_target_pairs={{0,32},{32,0},{64,96},{96,64},{128,160},{160,128},{192,224},{224,1... | collective-permute-start | bytes 4718600 | tf_op jit(solution)/shard_map/ppermute | solution.py:331
  20.5 8.1 %collective-permute-start.1 = (bf16[8,64,128]{2,1,0:T(8,128)(2,1)S(1)}, bf16[8,64,128]{2,1,0:T(8,128)(2,1)S(1)}, u32[]{:S(2)}, u32[]{:S(2)}) collective-permute-start(bf16[8,64,128]{2,1,0:T(8,128)(2,1)S(1)} %bitcast.17), channel_id=1, source_target_pairs={{0,12},{4,0},{8,4},{12,8},{16,28},{20,16},{24,20},{28,24},{1,13},{... | collective-permute-start | bytes 393224 | tf_op jit(solution)/shard_map/ppermute | solution.py:368
  26.5 23.9 %collective-permute-start.7 = (f32[64,128]{1,0:T(8,128)S(1)}, f32[64,128]{1,0:T(8,128)S(1)}, u32[]{:S(2)}, u32[]{:S(2)}) collective-permute-start(f32[64,128]{1,0:T(8,128)S(1)} %get-tuple-element.22), channel_id=1, source_target_pairs={{0,32},{32,0},{64,96},{96,64},{128,160},{160,128},{192,224},{224,1... | collective-permute-start | bytes 98312 | tf_op jit(solution)/shard_map/ppermute | solution.py:355
  27.4 1.9 %copy-start.3 = (bf16[3072,256]{1,0:T(8,128)(2,1)S(1)}, bf16[3072,256]{1,0:T(8,128)(2,1)}, u32[]{:S(2)}) copy-start(bf16[3072,256]{1,0:T(8,128)(2,1)} %v_ref.9) | copy-start | bytes 4718596
  27.4 7.3 %collective-permute-start.3 = (bf16[8,64,128]{2,1,0:T(8,128)(2,1)S(1)}, bf16[8,64,128]{2,1,0:T(8,128)(2,1)S(1)}, u32[]{:S(2)}, u32[]{:S(2)}) collective-permute-start(bf16[8,64,128]{2,1,0:T(8,128)(2,1)S(1)} %bitcast.18), channel_id=1, source_target_pairs={{0,8},{4,12},{8,0},{12,4},{16,24},{20,28},{24,16},{28,20},{1,9},{5... | collective-permute-start | bytes 393224 | tf_op jit(solution)/shard_map/ppermute | solution.py:368
  27.9 13.0 %collective-permute-start.5 = (bf16[8,64,128]{2,1,0:T(8,128)(2,1)S(1)}, bf16[8,64,128]{2,1,0:T(8,128)(2,1)S(1)}, u32[]{:S(2)}, u32[]{:S(2)}) collective-permute-start(bf16[8,64,128]{2,1,0:T(8,128)(2,1)S(1)} %bitcast.19), channel_id=1, source_target_pairs={{0,4},{4,8},{8,12},{12,0},{16,20},{20,24},{24,28},{28,16},{1,5},{5... | collective-permute-start | bytes 393224 | tf_op jit(solution)/shard_map/ppermute | solution.py:368
  33.5 17.0 %collective-permute-start.2 = (bf16[528,128]{1,0:T(8,128)(2,1)S(1)}, bf16[528,128]{1,0:T(8,128)(2,1)S(1)}, u32[]{:S(2)}, u32[]{:S(2)}) collective-permute-start(bf16[528,128]{1,0:T(8,128)(2,1)S(1)} %attend.5), channel_id=1, source_target_pairs={{0,4},{4,8},{8,12},{12,0},{16,20},{20,24},{24,28},{28,16},{1,5},{5... | collective-permute-start | bytes 405512 | tf_op jit(solution)/shard_map/ppermute | solution.py:373
  39.1 11.4 %collective-permute-start.4 = (bf16[528,128]{1,0:T(8,128)(2,1)S(1)}, bf16[528,128]{1,0:T(8,128)(2,1)S(1)}, u32[]{:S(2)}, u32[]{:S(2)}) collective-permute-start(bf16[528,128]{1,0:T(8,128)(2,1)S(1)} %attend.6), channel_id=1, source_target_pairs={{0,8},{4,12},{8,0},{12,4},{16,24},{20,28},{24,16},{28,20},{1,9},{5... | collective-permute-start | bytes 405512 | tf_op jit(solution)/shard_map/ppermute | solution.py:373
  45.3 5.3 %collective-permute-start.6 = (bf16[528,128]{1,0:T(8,128)(2,1)S(1)}, bf16[528,128]{1,0:T(8,128)(2,1)S(1)}, u32[]{:S(2)}, u32[]{:S(2)}) collective-permute-start(bf16[528,128]{1,0:T(8,128)(2,1)S(1)} %attend.7), channel_id=1, source_target_pairs={{0,12},{4,0},{8,4},{12,8},{16,28},{20,16},{24,20},{28,24},{1,13},{... | collective-permute-start | bytes 405512 | tf_op jit(solution)/shard_map/ppermute | solution.py:373
  50.5 11.2 %copy-start.4 = (bf16[2048,80]{0,1:T(8,128)(2,1)S(1)}, bf16[2048,80]{0,1:T(8,128)(2,1)}, u32[]{:S(2)}) copy-start(bf16[2048,80]{0,1:T(8,128)(2,1)} %param.17) | copy-start | bytes 983044
  51.5 3.9 %collective-permute-start.8 = (bf16[528,128]{1,0:T(8,128)(2,1)S(1)}, bf16[528,128]{1,0:T(8,128)(2,1)S(1)}, u32[]{:S(2)}, u32[]{:S(2)}) collective-permute-start(bf16[528,128]{1,0:T(8,128)(2,1)S(1)} %merge.1.a_ref), channel_id=1, source_target_pairs={{0,16},{32,48},{16,0},{48,32},{64,80},{96,112},{80,64},{112,96},{1... | collective-permute-start | bytes 405512 | tf_op jit(solution)/shard_map/ppermute | solution.py:378
  55.8 5.2 %collective-permute-start.9 = (bf16[528,128]{1,0:T(8,128)(2,1)S(1)}, bf16[528,128]{1,0:T(8,128)(2,1)S(1)}, u32[]{:S(2)}, u32[]{:S(2)}) collective-permute-start(bf16[528,128]{1,0:T(8,128)(2,1)S(1)} %pair.2.a_ref), channel_id=1, source_target_pairs={{0,208},{32,240},{16,64},{48,96},{64,16},{96,48},{80,128},{112,160... | collective-permute-start | bytes 405512 | tf_op jit(solution)/shard_map/ppermute | solution.py:378
  61.2 6.3 %collective-permute-start.10 = (bf16[528,128]{1,0:T(8,128)(2,1)S(1)}, bf16[528,128]{1,0:T(8,128)(2,1)S(1)}, u32[]{:S(2)}, u32[]{:S(2)}) collective-permute-start(bf16[528,128]{1,0:T(8,128)(2,1)S(1)} %pair.3.a_ref), channel_id=1, source_target_pairs={{0,80},{32,112},{16,192},{48,224},{64,144},{96,176},{80,0},{112,32... | collective-permute-start | bytes 405512 | tf_op jit(solution)/shard_map/ppermute | solution.py:380
  61.7 8.8 %collective-permute-start.14 = (bf16[80,1024]{1,0:T(8,128)(2,1)S(1)}, bf16[80,1024]{1,0:T(8,128)(2,1)S(1)}, u32[]{:S(2)}, u32[]{:S(2)}) collective-permute-start(bf16[80,1024]{1,0:T(8,128)(2,1)S(1)} %dynamic-slice_bitcast_fusion), channel_id=1, source_target_pairs={{0,32},{32,0},{64,96},{96,64},{128,160},{160,128},{192,224},{224,1... | collective-permute-start | bytes 491528 | tf_op jit(solution)/shard_map/ppermute | solution.py:336
  67.9 4.0 %collective-permute-start.11 = (bf16[64,1024]{1,0:T(8,128)(2,1)S(1)}, bf16[64,1024]{1,0:T(8,128)(2,1)S(1)}, u32[]{:S(2)}, u32[]{:S(2)}) collective-permute-start(bf16[64,1024]{1,0:T(8,128)(2,1)S(1)} %finish.1.a_ref), channel_id=1, source_target_pairs={{0,12},{4,0},{8,4},{12,8},{16,28},{20,16},{24,20},{28,24},{1,13},{... | collective-permute-start | bytes 393224 | tf_op jit(solution)/shard_map/ppermute | solution.py:383
  68.7 5.3 %collective-permute-start.12 = (bf16[64,1024]{1,0:T(8,128)(2,1)S(1)}, bf16[64,1024]{1,0:T(8,128)(2,1)S(1)}, u32[]{:S(2)}, u32[]{:S(2)}) collective-permute-start(bf16[64,1024]{1,0:T(8,128)(2,1)S(1)} %finish.1.a_ref), channel_id=1, source_target_pairs={{0,8},{4,12},{8,0},{12,4},{16,24},{20,28},{24,16},{28,20},{1,9},{5... | collective-permute-start | bytes 393224 | tf_op jit(solution)/shard_map/ppermute | solution.py:383
  70.5 5.0 %collective-permute-start.13 = (bf16[64,1024]{1,0:T(8,128)(2,1)S(1)}, bf16[64,1024]{1,0:T(8,128)(2,1)S(1)}, u32[]{:S(2)}, u32[]{:S(2)}) collective-permute-start(bf16[64,1024]{1,0:T(8,128)(2,1)S(1)} %finish.1.a_ref), channel_id=1, source_target_pairs={{0,4},{4,8},{8,12},{12,0},{16,20},{20,24},{24,28},{28,16},{1,5},{5... | collective-permute-start | bytes 393224 | tf_op jit(solution)/shard_map/ppermute | solution.py:383
  76.0 9.0 %collective-permute-start.15 = (bf16[4,4,16,80]{3,2,1,0:T(8,128)(2,1)S(1)}, bf16[4,4,16,80]{3,2,1,0:T(8,128)(2,1)S(1)}, u32[]{:S(2)}, u32[]{:S(2)}) collective-permute-start(bf16[4,4,16,80]{3,2,1,0:T(8,128)(2,1)S(1)} %get-tuple-element.24), channel_id=1, source_target_pairs={{0,32},{32,0},{64,96},{96,64},{128,160},{160,128},{192,224},{224,1... | collective-permute-start | bytes 122888 | tf_op jit(solution)/shard_map/ppermute | solution.py:395
  85.1 2.9 %collective-permute-start.16 = (bf16[2,4,16,80]{3,2,1,0:T(8,128)(2,1)S(1)}, bf16[2,4,16,80]{3,2,1,0:T(8,128)(2,1)S(1)}, u32[]{:S(2)}, u32[]{:S(2)}) collective-permute-start(bf16[2,4,16,80]{3,2,1,0:T(8,128)(2,1)S(1)} %get-tuple-element.26), channel_id=1, source_target_pairs={{0,1},{1,0},{2,3},{3,2},{4,5},{5,4},{6,7},{7,6},{8,9},{9,8},{10,11... | collective-permute-start | bytes 61448 | tf_op jit(solution)/shard_map/ppermute | solution.py:399
  87.9 4.0 %collective-permute-start.17 = (bf16[4,16,80]{2,1,0:T(8,128)(2,1)S(1)}, bf16[4,16,80]{2,1,0:T(8,128)(2,1)S(1)}, u32[]{:S(2)}, u32[]{:S(2)}) collective-permute-start(bf16[4,16,80]{2,1,0:T(8,128)(2,1)S(1)} %get-tuple-element.28), channel_id=1, source_target_pairs={{0,3},{1,2},{2,1},{3,0},{4,7},{5,6},{6,5},{7,4},{8,11},{9,10},{10,... | collective-permute-start | bytes 30728 | tf_op jit(solution)/shard_map/ppermute | solution.py:403
  (5 other events, 5.6 us)

commit v2 on v1

--- a/solution.py
+++ b/solution.py
@@ -48,6 +48,12 @@
     return [(zl * 4 + x, zl * 4 + (x + k) % 4) for zl in range(2) for x in range(4)]
 
 
+OUT_GROUPS = [
+    [plane_index(x, z, c) * 4 + t for x in range(NX) for c in range(2) for t in range(4)]
+    for z in range(NZ)
+]
+
+
 ROWS = NZ * 64
 PACKED = (ROWS + 16, HEAD)
 
@@ -56,13 +62,21 @@
     return lax.broadcasted_iota(jnp.int32, (HEAD, HEAD), 0) == lax.broadcasted_iota(
         jnp.int32, (HEAD, HEAD), 1
     )
+
+
+def to_row(column):
+    half = lax.broadcasted_iota(jnp.int32, (64, HEAD), 0)
+    lane = lax.broadcasted_iota(jnp.int32, (64, HEAD), 1)
+    low = jnp.where(half == lane, column[0:64], 0.0)
+    high = jnp.where(half + 64 == lane, column[64:128], 0.0)
+    return jnp.sum(low + high, axis=0, keepdims=True)
 
 
 def pack(o_ref, parts):
     rows = []
     for i, (out, lse) in enumerate(parts):
         o_ref[i * HEAD : (i + 1) * HEAD, :] = out.astype(BF16)
-        rows.append(jnp.sum(jnp.where(eye(), lse, 0.0), axis=0, keepdims=True))
+        rows.append(to_row(lse))
     rows = jnp.concatenate(rows, axis=0)
     high = rows.astype(BF16).astype(F32)
     middle = (rows - high).astype(BF16).astype(F32)
@@ -98,18 +112,27 @@
         o_ref[z] = rows
 
 
-def arrange_kernel(core_ref, k_ref, v_ref, send_ref, sems):
-    columns = pl.ds(pl.multiple_of((1 - core_ref[0]) * HEAD, HEAD), HEAD)
-    copies = [
-        pltpu.make_async_copy(
-            ref.at[:, columns], send_ref.at[:, pl.ds(i * HEAD, HEAD)], sems.at[i]
-        )
-        for i, ref in enumerate((k_ref, v_ref))
+def arrange_kernel(core_ref, k_ref, v_ref, w_ref, send_ref, mine_ref, other_ref, sems):
+    core = core_ref[0]
+    width = mine_ref.shape[1]
+    columns = pl.ds(pl.multiple_of((1 - core) * HEAD, HEAD), HEAD)
+    pairs = [
+        (k_ref.at[:, columns], send_ref.at[:, pl.ds(0, HEAD)]),
+        (v_ref.at[:, columns], send_ref.at[:, pl.ds(HEAD, HEAD)]),
+        (w_ref.at[:, pl.ds(pl.multiple_of(core * width, width), width)], mine_ref),
+        (w_ref.at[:, pl.ds(pl.multiple_of((1 - core) * width, width), width)], other_ref),
     ]
+    copies = [pltpu.make_async_copy(*pair, sems.at[i]) for i, pair in enumerate(pairs)]
     for copy in copies:
         copy.start()
     for copy in copies:
         copy.wait()
+
+
+def stack_kernel(a_ref, b_ref, o_ref):
+    rows = a_ref.shape[0]
+    o_ref[:rows] = a_ref[...]
+    o_ref[rows:] = b_ref[...]
 
 
 def suffix_kernel(length_ref, core_ref, q_ref, k_ref, v_ref, nk_ref, nv_ref, own_ref, send_ref):
@@ -202,7 +225,7 @@
     pack(o_ref, [merge(list(parts)) for parts in zip(unpack(a_ref), unpack(b_ref))])
 
 
-def finish_kernel(a_ref, b_ref, o_ref):
+def finish(a_ref, b_ref):
     rows = []
     for parts in zip(unpack(a_ref), unpack(b_ref)):
         out, _ = merge(list(parts))
@@ -218,39 +241,30 @@
                 for h in range(8)
             ]
             rows.append(jnp.concatenate(heads, axis=1))
-    o_ref[...] = jnp.concatenate(rows, axis=0).astype(BF16)
-
-
-def project_kernel(x_ref, core_ref, a_ref, b_ref, c_ref, d_ref, w_ref, ws_ref, own_ref, send_ref):
+    return jnp.concatenate(rows, axis=0).astype(BF16)
+
+
+def project_kernel(x_ref, core_ref, a_ref, b_ref, *refs):
+    *refs, o_ref = refs
     nt = (((1,), (1,)), ((), ()))
-    width = ws_ref.shape[1]
-    mine = w_ref[:, pl.ds(pl.multiple_of(core_ref[0] * width, width), width)]
-    other = ws_ref[...]
-    for k, ref in enumerate((a_ref, b_ref, c_ref, d_ref)):
+    rows = finish(a_ref, b_ref)
+    width = refs[0].shape[0] // 2
+    for k, ref in enumerate(refs):
         place = lax.rem(x_ref[0] + k, NX)
-        rows = ref[...]
-        for weight, o_ref in ((mine, own_ref), (other, send_ref)):
+        for half, owner in enumerate((core_ref[0], 1 - core_ref[0])):
+            weight = ref[half * width : (half + 1) * width, :]
             product = lax.dot_general(rows, weight, nt, preferred_element_type=F32)
             product = product.astype(BF16)
             for t in range(4):
-                o_ref[t, place] = product[t * 16 : (t + 1) * 16]
-
-
-def halve_kernel(t_ref, a_ref, b_ref, keep_ref, send_ref):
-    t = t_ref[0]
-    partner = t + 1 - 2 * lax.rem(t, 2)
-    for ref, owner in ((keep_ref, t), (send_ref, partner)):
-        for i, block in enumerate((owner, 3 - owner)):
-            ref[i] = (a_ref[block].astype(F32) + b_ref[block].astype(F32)).astype(BF16)
-
-
-def quarter_kernel(a_ref, b_ref, keep_ref, send_ref):
-    keep_ref[...] = a_ref[0].astype(F32) + b_ref[0].astype(F32)
-    send_ref[...] = (a_ref[1].astype(F32) + b_ref[1].astype(F32)).astype(BF16)
-
-
-def sum_kernel(a_ref, b_ref, o_ref):
-    total = (a_ref[...] + b_ref[...].astype(F32)).reshape(64, a_ref.shape[2])
+                o_ref[place, owner, t] = product[t * 16 : (t + 1) * 16]
+
+
+def sum_kernel(terms_ref, o_ref):
+    total = []
+    for x in range(NX):
+        terms = [terms_ref[x * 8 + k].astype(F32) for k in range(8)]
+        total.append(functools.reduce(jnp.add, terms))
+    total = jnp.concatenate(total, axis=0)
     row = lax.broadcasted_iota(jnp.int32, (64, 64), 0)
     column = lax.broadcasted_iota(jnp.int32, (64, 64), 1)
     source = (row % 4) * 16 + ((row // 4) % 2) * 8 + ((row // 8) % 2) * 4 + row // 16
@@ -292,7 +306,6 @@
     core = lax.rem(lax.axis_index("prefix"), 2).reshape(1)
     x = lax.rem(lax.axis_index("replica"), NX).reshape(1)
     z = (lax.axis_index("prefix") // 2 * 2 + lax.axis_index("replica") // NX).reshape(1)
-    tensor = lax.axis_index("tensor").reshape(1)
     kv_rows = common_prefix_keys.shape[0]
     slots = branch_suffix_keys.shape[1]
 
@@ -308,18 +321,19 @@
         axis_index_groups=ZC_GROUPS,
     ).reshape(NZ, 64, HEAD)
 
-    send = pl.pallas_call(
+    columns, width = out_weight.shape[1], out_weight.shape[0] // 2
+    send, weight_mine, weight_send = pl.pallas_call(
         arrange_kernel,
-        out_shape=shape((kv_rows, 2 * HEAD)),
-        in_specs=[SMEM] + [pl.BlockSpec(memory_space=pltpu.HBM)] * 2,
-        out_specs=pl.BlockSpec(memory_space=pltpu.HBM),
-        scratch_shapes=[pltpu.SemaphoreType.DMA((2,))],
+        out_shape=[shape((kv_rows, 2 * HEAD))] + [shape((columns, width))] * 2,
+        in_specs=[SMEM] + [pl.BlockSpec(memory_space=pltpu.HBM)] * 3,
+        out_specs=[pl.BlockSpec(memory_space=pltpu.HBM)] + [VMEM] * 2,
+        scratch_shapes=[pltpu.SemaphoreType.DMA((4,))],
         compiler_params=params(),
         cost_estimate=pl.CostEstimate(
             flops=0, bytes_accessed=kv_rows * HEAD * 8, transcendentals=0
         ),
         name="arrange",
-    )(core, common_prefix_keys, common_prefix_values)
+    )(core, common_prefix_keys, common_prefix_values, out_weight.T)
     near_queries, send = lax.optimization_barrier((near_queries, send))
     other = call(
         fetch_kernel,
@@ -330,10 +344,10 @@
         scratch=[pltpu.SemaphoreType.DMA],
     )(lax.ppermute(send, "prefix", CORE_SWAP))
 
-    weight = out_weight.T
-    width = weight.shape[1] // 2
-    weight_send = lax.dynamic_slice_in_dim(weight, (1 - core[0]) * width, width, 1)
-    weight_other = lax.ppermute(weight_send, "prefix", CORE_SWAP)
+    weight = call(stack_kernel, shape((2 * columns, width)), [VMEM] * 2, "stack")(
+        weight_mine, lax.ppermute(weight_send, "prefix", CORE_SWAP)
+    )
+    weights = [weight] + [lax.ppermute(weight, "replica", x_shift(-k)) for k in (1, 2, 3)]
 
     own, own_send = call(
         suffix_kernel,
@@ -355,7 +369,7 @@
     sibling = lax.ppermute(own_send, "prefix", CORE_SWAP)
 
     attend = call(
-        functools.partial(attend_kernel, 512),
+        functools.partial(attend_kernel, 256),
         shape(PACKED),
         [SMEM] + [VMEM] * 4,
         "attend",
@@ -378,30 +392,23 @@
         arrived = lax.ppermute(merged, PLANE, z_exchange(step))
         merged = call(pair_kernel, shape(PACKED), [VMEM] * 2, "pair")(merged, arrived)
     arrived = lax.ppermute(merged, PLANE, z_exchange(2))
-    near_rows = call(finish_kernel, shape((64, 1024)), [VMEM] * 2, "finish")(merged, arrived)
-    chunk_rows = [near_rows] + [
-        lax.ppermute(near_rows, "replica", x_shift(-k)) for k in (1, 2, 3)
-    ]
-    columns = out_weight.shape[1]
-    block = (NX, 16, columns)
-    product, product_send = call(
+    product = call(
         project_kernel,
-        [shape((4,) + block)] * 2,
+        shape((NX, 2, 4, 16, columns)),
         [SMEM] * 2 + [VMEM] * 6,
         "project",
-        flops=2 * 256 * 1024 * 160,
-        moved=1 << 20,
-    )(x, core, *chunk_rows, weight, weight_other)
-    product_other = lax.ppermute(product_send, "prefix", CORE_SWAP)
-    kept, sent = call(
-        halve_kernel, [shape((2,) + block)] * 2, [SMEM] + [VMEM] * 2, "halve"
-    )(tensor, product, product_other)
-    arrived = lax.ppermute(sent, "tensor", [(t, t ^ 1) for t in range(4)])
-    kept, sent = call(
-        quarter_kernel, [shape(block, F32), shape(block)], [VMEM] * 2, "quarter"
-    )(kept, arrived)
-    arrived = lax.ppermute(sent, "tensor", [(t, 3 - t) for t in range(4)])
-    return call(sum_kernel, shape((4, 16, columns)), [VMEM] * 2, "sum")(kept, arrived)
+        flops=2 * 64 * 1024 * 640,
+        moved=2 << 20,
+    )(x, core, merged, arrived, *weights)
+    terms = lax.all_to_all(
+        product.reshape(NX * 8, 16, columns),
+        PLANE + ("tensor",),
+        0,
+        0,
+        tiled=True,
+        axis_index_groups=OUT_GROUPS,
+    )
+    return call(sum_kernel, shape((4, 16, columns)), [VMEM], "sum")(terms)
 
 
 def solution(mesh):

time: 94.1 us -> 86.8 us (0.922); the launches traced: 92.7 us -> 86.4 us
  blocking collectives: 0 us -> 17.1 us
  starting transfers between devices: 38.2 us -> 22.1 us
  waiting for transfers between devices: 25.3 us -> 18.2 us
    all_to_all x0 -> x1, blocking collectives: none -> 17.1 us  [local(): lax.all_to_all(product.reshape(NX * 8, 16, columns), PLANE + ('tensor',),...]
    ppermute x7 -> x4, starting transfers between devices: 19 us -> 2.75 us  [the longest x3 2.65 us: local(): lax.ppermute(weight, 'replica', x_shift(-k))]
    ppermute x2, waiting for transfers between devices: 8.84 us -> 6.41 us  [local(): arrived = lax.ppermute(merged, PLANE, z_exchange(step))]
    all_to_all x1, waiting for transfers between devices: 6.05 us -> 3.78 us  [local(): lax.all_to_all(query_rows.reshape(2 * NZ, 32, HEAD), PLANE, 0, 0, tiled=T...]
    ppermute x1, waiting for transfers between devices: 1.85 us -> 0.01 us  [local(): arrived = lax.ppermute(merged, PLANE, z_exchange(2))]
    ppermute x7 -> x4, waiting for transfers between devices: 8.52 us -> 8.03 us  [the longest x3 8.03 us: local(): lax.ppermute(weight, 'replica', x_shift(-k))]
    unnamed x20 -> x22, local copies, waits for them, and re-layouts: 6.23 us -> 6.32 us
  transfers between devices with their start and end apart: 19 -> 16, of which waited for: 10 -> 4; matrix products, arithmetic and copies ran while one was open for 0% -> 0% of each run, Pallas kernels for 20% -> 23%
where the time goes in v2:
time: 86.8 us; the launch traced here: 86.4 us
  starting transfers between devices  22.1 us (25%)
  Pallas kernels  21.9 us (25%)
  waiting for transfers between devices  18.2 us (21%)
  blocking collectives  17.1 us (20%)
  local copies, waits for them, and re-layouts  6.32 us (7%)
    all_to_all x1, blocking collectives, local(): lax.all_to_all(product.reshape(NX * 8, 16, columns), PLANE + ('tensor',),...  17.1 us
    pallas_call x4, Pallas kernels, local(): attend(core, q, common_prefix_keys, common_prefix_values, other)  17 us
    all_to_all x1, starting transfers between devices, local(): lax.all_to_all(query_rows.reshape(2 * NZ, 32, HEAD), PLANE, 0, 0, tiled=T...  9.98 us
    ppermute x3, waiting for transfers between devices, local(): lax.ppermute(weight, 'replica', x_shift(-k))  8.03 us
    ppermute x2, waiting for transfers between devices, local(): arrived = lax.ppermute(merged, PLANE, z_exchange(step))  6.41 us
    unnamed x22, local copies, waits for them, and re-layouts  6.32 us
    ppermute x3, starting transfers between devices, local(): back = [lax.ppermute(partial[k], 'replica', x_shift(k)) for k in (1, 2, 3)]  3.99 us
    all_to_all x1, waiting for transfers between devices, local(): lax.all_to_all(query_rows.reshape(2 * NZ, 32, HEAD), PLANE, 0, 0, tiled=T...  3.78 us
  transfers between devices with their start and end apart: 16, of which 4 were waited for; matrix products, arithmetic and copies ran while one was open for 0% of the time, Pallas kernels for 23%

profile of v2, /device:TPU:1, one launch (start us, length us, event | category | flops | bytes accessed | tf_op | source)
XLA Modules:
  0.0 86.4 jit_solution(744628091846600891)
XLA Ops:
  1.4 10.0 %all-to-all-start = ((bf16[16,32,128]{2,1,0:T(8,128)(2,1)}), bf16[16,32,128]{2,1,0:T(8,128)(2,1)S(1)}, u32[]{:S(2)}, u32[]{:S(2)}) async-start(bf16[16,32,128]{2,1,0:T(8,128)(2,1)} %bitcast.4), calls=%async_computation | async-start | bytes 262144 | tf_op jit(solution)/shard_map/all_to_all | solution.py:315
  11.4 1.4 %copy-done = bf16[3072,256]{1,0:T(8,128)(2,1)S(1)} copy-done((bf16[3072,256]{1,0:T(8,128)(2,1)S(1)}, bf16[3072,256]{1,0:T(8,128)(2,1)}, u32[]{:S(2)}) %copy-start) | copy-done | bytes 1572888
  12.8 1.4 %copy-done.2 = bf16[3072,256]{1,0:T(8,128)(2,1)S(1)} copy-done((bf16[3072,256]{1,0:T(8,128)(2,1)S(1)}, bf16[3072,256]{1,0:T(8,128)(2,1)}, u32[]{:S(2)}) %copy-start.2) | copy-done | bytes 1572888
  14.2 1.0 %copy-done.6 = bf16[2048,80]{0,1:T(8,128)(2,1)S(1)} copy-done((bf16[2048,80]{0,1:T(8,128)(2,1)S(1)}, bf16[2048,80]{0,1:T(8,128)(2,1)}, u32[]{:S(2)}) %copy-start.6) | copy-done | bytes 327704
  15.6 1.2 %copy-done.10 = bf16[3072,256]{1,0:T(8,128)(2,1)} copy-done((bf16[3072,256]{1,0:T(8,128)(2,1)}, bf16[3072,256]{1,0:T(8,128)(2,1)S(1)}, u32[]{:S(2)}) %copy-start.10) | copy-done | bytes 1572888
  16.8 3.8 %all-to-all-done = bf16[16,32,128]{2,1,0:T(8,128)(2,1)S(1)} async-done(((bf16[16,32,128]{2,1,0:T(8,128)(2,1)}), bf16[16,32,128]{2,1,0:T(8,128)(2,1)S(1)}, u32[]{:S(2)}, u32[]{:S(2)}) %all-to-all-start) | async-done | bytes 131104 | tf_op jit(solution)/shard_map/all_to_all | solution.py:315
  20.6 2.5 %collective-permute-start.1 = (bf16[8,64,128]{2,1,0:T(8,128)(2,1)S(1)}, bf16[8,64,128]{2,1,0:T(8,128)(2,1)S(1)}, u32[]{:S(2)}, u32[]{:S(2)}) collective-permute-start(bf16[8,64,128]{2,1,0:T(8,128)(2,1)S(1)} %bitcast.16), channel_id=1, source_target_pairs={{0,12},{4,0},{8,4},{12,8},{16,28},{20,16},{24,20},{28,24},{1,13},{... | collective-permute-start | bytes 393224 | tf_op jit(solution)/shard_map/ppermute | solution.py:382
  23.7 0.8 suffix.1
  24.5 0.9 %collective-permute-start.7 = (f32[64,128]{1,0:T(8,128)S(1)}, f32[64,128]{1,0:T(8,128)S(1)}, u32[]{:S(2)}, u32[]{:S(2)}) collective-permute-start(f32[64,128]{1,0:T(8,128)S(1)} %get-tuple-element.20), channel_id=1, source_target_pairs={{0,32},{32,0},{64,96},{96,64},{128,160},{160,128},{192,224},{224,1... | collective-permute-start | bytes 98312 | tf_op jit(solution)/shard_map/ppermute | solution.py:369
  27.4 4.2 %attend.5 = bf16[528,128]{1,0:T(8,128)(2,1)S(1)} custom-call(s32[1]{0:T(128)} %bitcast.1.core_ref, bf16[8,64,128]{2,1,0:T(8,128)(2,1)S(1)} %collective-permute-done.1.q_ref, bf16[3072,256]{1,0:T(8,128)(2,1)S(1)} %copy-done.1, bf16[3072,256]{1,0:T(8,128)(2,1)S(1)} %copy-done.3, bf16[3072,256]{1,0:T(8,128)(2,1)S(1)} %fetch.1.other_ref), custom_call_target="tpu_custom_call" | custom-call | flops 1610612736 | bytes 4718592 | tf_op jit(solution)/shard_map/attend/pallas_call | solution.py:385
  31.6 1.2 %collective-permute-start.2 = (bf16[528,128]{1,0:T(8,128)(2,1)S(1)}, bf16[528,128]{1,0:T(8,128)(2,1)S(1)}, u32[]{:S(2)}, u32[]{:S(2)}) collective-permute-start(bf16[528,128]{1,0:T(8,128)(2,1)S(1)} %attend.5), channel_id=1, source_target_pairs={{0,4},{4,8},{8,12},{12,0},{16,20},{20,24},{24,28},{28,16},{1,5},{5... | collective-permute-start | bytes 405512 | tf_op jit(solution)/shard_map/ppermute | solution.py:387
  32.8 4.4 %attend.6 = bf16[528,128]{1,0:T(8,128)(2,1)S(1)} custom-call(s32[1]{0:T(128)} %bitcast.1.core_ref, bf16[8,64,128]{2,1,0:T(8,128)(2,1)S(1)} %collective-permute-done.3.q_ref, bf16[3072,256]{1,0:T(8,128)(2,1)S(1)} %copy-done.1, bf16[3072,256]{1,0:T(8,128)(2,1)S(1)} %copy-done.3, bf16[3072,256]{1,0:T(8,128)(2,1)S(1)} %fetch.1.other_ref), custom_call_target="tpu_custom_call" | custom-call | flops 1610612736 | bytes 4718592 | tf_op jit(solution)/shard_map/attend/pallas_call | solution.py:385
  37.1 1.8 %collective-permute-start.4 = (bf16[528,128]{1,0:T(8,128)(2,1)S(1)}, bf16[528,128]{1,0:T(8,128)(2,1)S(1)}, u32[]{:S(2)}, u32[]{:S(2)}) collective-permute-start(bf16[528,128]{1,0:T(8,128)(2,1)S(1)} %attend.6), channel_id=1, source_target_pairs={{0,8},{4,12},{8,0},{12,4},{16,24},{20,28},{24,16},{28,20},{1,9},{5... | collective-permute-start | bytes 405512 | tf_op jit(solution)/shard_map/ppermute | solution.py:387
  38.9 4.2 %attend.7 = bf16[528,128]{1,0:T(8,128)(2,1)S(1)} custom-call(s32[1]{0:T(128)} %bitcast.1.core_ref, bf16[8,64,128]{2,1,0:T(8,128)(2,1)S(1)} %collective-permute-done.5.q_ref, bf16[3072,256]{1,0:T(8,128)(2,1)S(1)} %copy-done.1, bf16[3072,256]{1,0:T(8,128)(2,1)S(1)} %copy-done.3, bf16[3072,256]{1,0:T(8,128)(2,1)S(1)} %fetch.1.other_ref), custom_call_target="tpu_custom_call" | custom-call | flops 1610612736 | bytes 4718592 | tf_op jit(solution)/shard_map/attend/pallas_call | solution.py:385
  43.1 1.0 %collective-permute-start.6 = (bf16[528,128]{1,0:T(8,128)(2,1)S(1)}, bf16[528,128]{1,0:T(8,128)(2,1)S(1)}, u32[]{:S(2)}, u32[]{:S(2)}) collective-permute-start(bf16[528,128]{1,0:T(8,128)(2,1)S(1)} %attend.7), channel_id=1, source_target_pairs={{0,12},{4,0},{8,4},{12,8},{16,28},{20,16},{24,20},{28,24},{1,13},{... | collective-permute-start | bytes 405512 | tf_op jit(solution)/shard_map/ppermute | solution.py:387
  44.1 4.2 %attend.4.a_ref = bf16[528,128]{1,0:T(8,128)(2,1)S(1)} custom-call(s32[1]{0:T(128)} %bitcast.1.core_ref, bf16[8,64,128]{2,1,0:T(8,128)(2,1)S(1)} %bitcast.19, bf16[3072,256]{1,0:T(8,128)(2,1)S(1)} %copy-done.1, bf16[3072,256]{1,0:T(8,128)(2,1)S(1)} %copy-done.3, bf16[3072,256]{1,0:T(8,128)(2,1)S(1)} %fetch.1.other_ref), custom_call_target="tpu_custom_call" | custom-call | flops 1610612736 | bytes 4718592 | tf_op jit(solution)/shard_map/attend/pallas_call | solution.py:385
  48.4 1.0 %merge.1.a_ref = bf16[528,128]{1,0:T(8,128)(2,1)S(1)} custom-call(s32[1]{0:T(128)} %bitcast.2.z_ref, s32[1]{0:T(128)} %bitcast.1.core_ref, bf16[528,128]{1,0:T(8,128)(2,1)S(1)} %attend.4.a_ref, bf16[528,128]{1,0:T(8,128)(2,1)S(1)} %collective-permute-done.2.b_ref, bf16[528,128]{1,0:T(8,128)(2,1)S(1)} %collective-permute-done.4.c_ref, ...), custom_call_target="tpu_custom_call" | custom-call | bytes 811008 | tf_op jit(solution)/shard_map/merge/pallas_call | solution.py:388
  49.5 0.9 %collective-permute-start.12 = (bf16[160,1024]{1,0:T(8,128)(2,1)S(1)}, bf16[160,1024]{1,0:T(8,128)(2,1)S(1)}, u32[]{:S(2)}, u32[]{:S(2)}) collective-permute-start(bf16[160,1024]{1,0:T(8,128)(2,1)S(1)} %stack.1.refs_0_), channel_id=1, source_target_pairs={{0,12},{4,0},{8,4},{12,8},{16,28},{20,16},{24,20},{28,24},{1,13},{... | collective-permute-start | bytes 983048 | tf_op jit(solution)/shard_map/ppermute | solution.py:350
  50.5 1.7 %collective-permute-start.13 = (bf16[160,1024]{1,0:T(8,128)(2,1)S(1)}, bf16[160,1024]{1,0:T(8,128)(2,1)S(1)}, u32[]{:S(2)}, u32[]{:S(2)}) collective-permute-start(bf16[160,1024]{1,0:T(8,128)(2,1)S(1)} %stack.1.refs_0_), channel_id=1, source_target_pairs={{0,8},{4,12},{8,0},{12,4},{16,24},{20,28},{24,16},{28,20},{1,9},{5... | collective-permute-start | bytes 983048 | tf_op jit(solution)/shard_map/ppermute | solution.py:350
  52.2 1.1 %collective-permute-done.8.b_ref = bf16[528,128]{1,0:T(8,128)(2,1)S(1)} collective-permute-done((bf16[528,128]{1,0:T(8,128)(2,1)S(1)}, bf16[528,128]{1,0:T(8,128)(2,1)S(1)}, u32[]{:S(2)}, u32[]{:S(2)}) %collective-permute-start.8) | collective-permute-done | bytes 135200 | tf_op jit(solution)/shard_map/ppermute | solution.py:392
  53.8 5.3 %collective-permute-done.9.b_ref = bf16[528,128]{1,0:T(8,128)(2,1)S(1)} collective-permute-done((bf16[528,128]{1,0:T(8,128)(2,1)S(1)}, bf16[528,128]{1,0:T(8,128)(2,1)S(1)}, u32[]{:S(2)}, u32[]{:S(2)}) %collective-permute-start.9) | collective-permute-done | bytes 135200 | tf_op jit(solution)/shard_map/ppermute | solution.py:392
  59.9 8.0 %collective-permute-done.14.refs_3_ = bf16[160,1024]{1,0:T(8,128)(2,1)S(1)} collective-permute-done((bf16[160,1024]{1,0:T(8,128)(2,1)S(1)}, bf16[160,1024]{1,0:T(8,128)(2,1)S(1)}, u32[]{:S(2)}, u32[]{:S(2)}) %collective-permute-start.14) | collective-permute-done | bytes 327712 | tf_op jit(solution)/shard_map/ppermute | solution.py:350
  68.6 17.1 %all_to_all.10.terms_ref = bf16[32,16,80]{2,1,0:T(8,128)(2,1)S(1)} all-to-all(bf16[32,16,80]{2,1,0:T(8,128)(2,1)S(1)} %bitcast.14), channel_id=1, replica_groups={{0,1,2,3,32,33,34,35,4,5,6,7,36,37,38,39,8,9,10,11,40,41,42,43,12,13,14..., dimensions={0} | all-to-all | bytes 163840 | tf_op jit(solution)/shard_map/all_to_all | solution.py:403
  85.7 0.8 sum.1
  (45 shorter events, 6.0 us)
Async XLA Ops:
  1.4 19.1 %all-to-all-start = ((bf16[16,32,128]{2,1,0:T(8,128)(2,1)}), bf16[16,32,128]{2,1,0:T(8,128)(2,1)S(1)}, u32[]{:S(2)}, u32[]{:S(2)}) async-start(bf16[16,32,128]{2,1,0:T(8,128)(2,1)} %bitcast.4), calls=%async_computation | async-start | bytes 262144 | tf_op jit(solution)/shard_map/all_to_all | solution.py:315
  11.4 1.4 %copy-start = (bf16[3072,256]{1,0:T(8,128)(2,1)S(1)}, bf16[3072,256]{1,0:T(8,128)(2,1)}, u32[]{:S(2)}) copy-start(bf16[3072,256]{1,0:T(8,128)(2,1)} %k_ref.9) | copy-start | bytes 4718596
  12.8 1.4 %copy-start.2 = (bf16[3072,256]{1,0:T(8,128)(2,1)S(1)}, bf16[3072,256]{1,0:T(8,128)(2,1)}, u32[]{:S(2)}) copy-start(bf16[3072,256]{1,0:T(8,128)(2,1)} %v_ref.9) | copy-start | bytes 4718596
  15.2 8.5 %copy-start.4 = (bf16[1,1024,256]{2,1,0:T(8,128)(2,1)S(1)}, bf16[1,1024,256]{2,1,0:T(8,128)(2,1)}, u32[]{:S(2)}) copy-start(bf16[1,1024,256]{2,1,0:T(8,128)(2,1)} %param.12) | copy-start | bytes 1572868
  15.2 8.5 %copy-start.5 = (bf16[1,1024,256]{2,1,0:T(8,128)(2,1)S(1)}, bf16[1,1024,256]{2,1,0:T(8,128)(2,1)}, u32[]{:S(2)}) copy-start(bf16[1,1024,256]{2,1,0:T(8,128)(2,1)} %param.13) | copy-start | bytes 1572868
  15.2 8.5 %copy-start.8 = (bf16[4,1,256]{2,0,1:T(4,128)(2,1)S(1)}, bf16[4,1,256]{2,0,1:T(4,128)(2,1)}, u32[]{:S(2)}) copy-start(bf16[4,1,256]{2,0,1:T(4,128)(2,1)} %param.14) | copy-start | bytes 6148
  15.2 8.5 %copy-start.9 = (bf16[4,1,256]{2,0,1:T(4,128)(2,1)S(1)}, bf16[4,1,256]{2,0,1:T(4,128)(2,1)}, u32[]{:S(2)}) copy-start(bf16[4,1,256]{2,0,1:T(4,128)(2,1)} %param.15) | copy-start | bytes 6148
  20.6 5.4 %collective-permute-start = (bf16[3072,256]{1,0:T(8,128)(2,1)}, bf16[3072,256]{1,0:T(8,128)(2,1)S(1)}, u32[]{:S(2)}, u32[]{:S(2)}) collective-permute-start(bf16[3072,256]{1,0:T(8,128)(2,1)} %copy-done.10), channel_id=1, source_target_pairs={{0,32},{32,0},{64,96},{96,64},{128,160},{160,128},{192,224},{224,1... | collective-permute-start | bytes 4718600 | tf_op jit(solution)/shard_map/ppermute | solution.py:345
  20.6 6.2 %collective-permute-start.1 = (bf16[8,64,128]{2,1,0:T(8,128)(2,1)S(1)}, bf16[8,64,128]{2,1,0:T(8,128)(2,1)S(1)}, u32[]{:S(2)}, u32[]{:S(2)}) collective-permute-start(bf16[8,64,128]{2,1,0:T(8,128)(2,1)S(1)} %bitcast.16), channel_id=1, source_target_pairs={{0,12},{4,0},{8,4},{12,8},{16,28},{20,16},{24,20},{28,24},{1,13},{... | collective-permute-start | bytes 393224 | tf_op jit(solution)/shard_map/ppermute | solution.py:382
  24.5 23.8 %collective-permute-start.7 = (f32[64,128]{1,0:T(8,128)S(1)}, f32[64,128]{1,0:T(8,128)S(1)}, u32[]{:S(2)}, u32[]{:S(2)}) collective-permute-start(f32[64,128]{1,0:T(8,128)S(1)} %get-tuple-element.20), channel_id=1, source_target_pairs={{0,32},{32,0},{64,96},{96,64},{128,160},{160,128},{192,224},{224,1... | collective-permute-start | bytes 98312 | tf_op jit(solution)/shard_map/ppermute | solution.py:369
  25.4 24.1 %collective-permute-start.11 = (bf16[80,1024]{1,0:T(8,128)(2,1)S(1)}, bf16[80,1024]{1,0:T(8,128)(2,1)S(1)}, u32[]{:S(2)}, u32[]{:S(2)}) collective-permute-start(bf16[80,1024]{1,0:T(8,128)(2,1)S(1)} %get-tuple-element.22), channel_id=1, source_target_pairs={{0,32},{32,0},{64,96},{96,64},{128,160},{160,128},{192,224},{224,1... | collective-permute-start | bytes 491528 | tf_op jit(solution)/shard_map/ppermute | solution.py:348
  25.5 1.4 %copy-start.1 = (bf16[3072,256]{1,0:T(8,128)(2,1)S(1)}, bf16[3072,256]{1,0:T(8,128)(2,1)}, u32[]{:S(2)}) copy-start(bf16[3072,256]{1,0:T(8,128)(2,1)} %k_ref.9) | copy-start | bytes 4718596
  25.5 1.9 %copy-start.3 = (bf16[3072,256]{1,0:T(8,128)(2,1)S(1)}, bf16[3072,256]{1,0:T(8,128)(2,1)}, u32[]{:S(2)}) copy-start(bf16[3072,256]{1,0:T(8,128)(2,1)} %v_ref.9) | copy-start | bytes 4718596
  25.5 7.3 %collective-permute-start.3 = (bf16[8,64,128]{2,1,0:T(8,128)(2,1)S(1)}, bf16[8,64,128]{2,1,0:T(8,128)(2,1)S(1)}, u32[]{:S(2)}, u32[]{:S(2)}) collective-permute-start(bf16[8,64,128]{2,1,0:T(8,128)(2,1)S(1)} %bitcast.17), channel_id=1, source_target_pairs={{0,8},{4,12},{8,0},{12,4},{16,24},{20,28},{24,16},{28,20},{1,9},{5... | collective-permute-start | bytes 393224 | tf_op jit(solution)/shard_map/ppermute | solution.py:382
  26.0 12.9 %collective-permute-start.5 = (bf16[8,64,128]{2,1,0:T(8,128)(2,1)S(1)}, bf16[8,64,128]{2,1,0:T(8,128)(2,1)S(1)}, u32[]{:S(2)}, u32[]{:S(2)}) collective-permute-start(bf16[8,64,128]{2,1,0:T(8,128)(2,1)S(1)} %bitcast.18), channel_id=1, source_target_pairs={{0,4},{4,8},{8,12},{12,0},{16,20},{20,24},{24,28},{28,16},{1,5},{5... | collective-permute-start | bytes 393224 | tf_op jit(solution)/shard_map/ppermute | solution.py:382
  31.6 16.8 %collective-permute-start.2 = (bf16[528,128]{1,0:T(8,128)(2,1)S(1)}, bf16[528,128]{1,0:T(8,128)(2,1)S(1)}, u32[]{:S(2)}, u32[]{:S(2)}) collective-permute-start(bf16[528,128]{1,0:T(8,128)(2,1)S(1)} %attend.5), channel_id=1, source_target_pairs={{0,4},{4,8},{8,12},{12,0},{16,20},{20,24},{24,28},{28,16},{1,5},{5... | collective-permute-start | bytes 405512 | tf_op jit(solution)/shard_map/ppermute | solution.py:387
  37.1 11.2 %collective-permute-start.4 = (bf16[528,128]{1,0:T(8,128)(2,1)S(1)}, bf16[528,128]{1,0:T(8,128)(2,1)S(1)}, u32[]{:S(2)}, u32[]{:S(2)}) collective-permute-start(bf16[528,128]{1,0:T(8,128)(2,1)S(1)} %attend.6), channel_id=1, source_target_pairs={{0,8},{4,12},{8,0},{12,4},{16,24},{20,28},{24,16},{28,20},{1,9},{5... | collective-permute-start | bytes 405512 | tf_op jit(solution)/shard_map/ppermute | solution.py:387
  43.1 5.2 %collective-permute-start.6 = (bf16[528,128]{1,0:T(8,128)(2,1)S(1)}, bf16[528,128]{1,0:T(8,128)(2,1)S(1)}, u32[]{:S(2)}, u32[]{:S(2)}) collective-permute-start(bf16[528,128]{1,0:T(8,128)(2,1)S(1)} %attend.7), channel_id=1, source_target_pairs={{0,12},{4,0},{8,4},{12,8},{16,28},{20,16},{24,20},{28,24},{1,13},{... | collective-permute-start | bytes 405512 | tf_op jit(solution)/shard_map/ppermute | solution.py:387
  49.3 3.9 %collective-permute-start.8 = (bf16[528,128]{1,0:T(8,128)(2,1)S(1)}, bf16[528,128]{1,0:T(8,128)(2,1)S(1)}, u32[]{:S(2)}, u32[]{:S(2)}) collective-permute-start(bf16[528,128]{1,0:T(8,128)(2,1)S(1)} %merge.1.a_ref), channel_id=1, source_target_pairs={{0,16},{32,48},{16,0},{48,32},{64,80},{96,112},{80,64},{112,96},{1... | collective-permute-start | bytes 405512 | tf_op jit(solution)/shard_map/ppermute | solution.py:392
  49.5 10.4 %collective-permute-start.12 = (bf16[160,1024]{1,0:T(8,128)(2,1)S(1)}, bf16[160,1024]{1,0:T(8,128)(2,1)S(1)}, u32[]{:S(2)}, u32[]{:S(2)}) collective-permute-start(bf16[160,1024]{1,0:T(8,128)(2,1)S(1)} %stack.1.refs_0_), channel_id=1, source_target_pairs={{0,12},{4,0},{8,4},{12,8},{16,28},{20,16},{24,20},{28,24},{1,13},{... | collective-permute-start | bytes 983048 | tf_op jit(solution)/shard_map/ppermute | solution.py:350
  50.5 9.5 %collective-permute-start.13 = (bf16[160,1024]{1,0:T(8,128)(2,1)S(1)}, bf16[160,1024]{1,0:T(8,128)(2,1)S(1)}, u32[]{:S(2)}, u32[]{:S(2)}) collective-permute-start(bf16[160,1024]{1,0:T(8,128)(2,1)S(1)} %stack.1.refs_0_), channel_id=1, source_target_pairs={{0,8},{4,12},{8,0},{12,4},{16,24},{20,28},{24,16},{28,20},{1,9},{5... | collective-permute-start | bytes 983048 | tf_op jit(solution)/shard_map/ppermute | solution.py:350
  52.2 15.8 %collective-permute-start.14 = (bf16[160,1024]{1,0:T(8,128)(2,1)S(1)}, bf16[160,1024]{1,0:T(8,128)(2,1)S(1)}, u32[]{:S(2)}, u32[]{:S(2)}) collective-permute-start(bf16[160,1024]{1,0:T(8,128)(2,1)S(1)} %stack.1.refs_0_), channel_id=1, source_target_pairs={{0,4},{4,8},{8,12},{12,0},{16,20},{20,24},{24,28},{28,16},{1,5},{5... | collective-permute-start | bytes 983048 | tf_op jit(solution)/shard_map/ppermute | solution.py:350
  53.6 5.5 %collective-permute-start.9 = (bf16[528,128]{1,0:T(8,128)(2,1)S(1)}, bf16[528,128]{1,0:T(8,128)(2,1)S(1)}, u32[]{:S(2)}, u32[]{:S(2)}) collective-permute-start(bf16[528,128]{1,0:T(8,128)(2,1)S(1)} %pair.2.a_ref), channel_id=1, source_target_pairs={{0,208},{32,240},{16,64},{48,96},{64,16},{96,48},{80,128},{112,160... | collective-permute-start | bytes 405512 | tf_op jit(solution)/shard_map/ppermute | solution.py:392
  59.4 8.6 %collective-permute-start.10 = (bf16[528,128]{1,0:T(8,128)(2,1)S(1)}, bf16[528,128]{1,0:T(8,128)(2,1)S(1)}, u32[]{:S(2)}, u32[]{:S(2)}) collective-permute-start(bf16[528,128]{1,0:T(8,128)(2,1)S(1)} %pair.3.a_ref), channel_id=1, source_target_pairs={{0,80},{32,112},{16,192},{48,224},{64,144},{96,176},{80,0},{112,32... | collective-permute-start | bytes 405512 | tf_op jit(solution)/shard_map/ppermute | solution.py:394
  (3 other events, 2.9 us)

commit v3 on v2

--- a/solution.py
+++ b/solution.py
@@ -49,8 +49,9 @@
 
 
 OUT_GROUPS = [
-    [plane_index(x, z, c) * 4 + t for x in range(NX) for c in range(2) for t in range(4)]
+    [plane_index(x, z, c) * 4 + t for x in range(NX) for t in range(4)]
     for z in range(NZ)
+    for c in range(2)
 ]
 
 
@@ -103,8 +104,11 @@
     return summed / total, top + jnp.log2(total)
 
 
-def query_kernel(q_ref, o_ref, flat_ref):
-    q = q_ref[...].astype(F32)
+def query_kernel(q_ref, o_ref, flat_ref, held_ref, sem):
+    copy = pltpu.make_async_copy(q_ref, held_ref, sem)
+    copy.start()
+    copy.wait()
+    q = held_ref[...].reshape(4, 16 * HEAD).astype(F32)
     rows = jnp.concatenate([q[:, i * HEAD : (i + 1) * HEAD] for i in range(16)], axis=0)
     rows = rows.astype(BF16)
     flat_ref[...] = rows
@@ -244,25 +248,29 @@
     return jnp.concatenate(rows, axis=0).astype(BF16)
 
 
-def project_kernel(x_ref, core_ref, a_ref, b_ref, *refs):
-    *refs, o_ref = refs
+def project_kernel(x_ref, a_ref, b_ref, *refs):
+    *refs, own_ref, send_ref = refs
     nt = (((1,), (1,)), ((), ()))
     rows = finish(a_ref, b_ref)
     width = refs[0].shape[0] // 2
     for k, ref in enumerate(refs):
         place = lax.rem(x_ref[0] + k, NX)
-        for half, owner in enumerate((core_ref[0], 1 - core_ref[0])):
+        for half, o_ref in enumerate((own_ref, send_ref)):
             weight = ref[half * width : (half + 1) * width, :]
             product = lax.dot_general(rows, weight, nt, preferred_element_type=F32)
             product = product.astype(BF16)
             for t in range(4):
-                o_ref[place, owner, t] = product[t * 16 : (t + 1) * 16]
+                o_ref[place, t] = product[t * 16 : (t + 1) * 16]
+
+
+def add_kernel(a_ref, b_ref, o_ref):
+    o_ref[...] = (a_ref[...].astype(F32) + b_ref[...].astype(F32)).astype(BF16)
 
 
 def sum_kernel(terms_ref, o_ref):
     total = []
     for x in range(NX):
-        terms = [terms_ref[x * 8 + k].astype(F32) for k in range(8)]
+        terms = [terms_ref[x * 4 + k].astype(F32) for k in range(4)]
         total.append(functools.reduce(jnp.add, terms))
     total = jnp.concatenate(total, axis=0)
     row = lax.broadcasted_iota(jnp.int32, (64, 64), 0)
@@ -310,8 +318,12 @@
     slots = branch_suffix_keys.shape[1]
 
     query_rows, query_flat = call(
-        query_kernel, [shape((NZ, 64, HEAD)), shape((64, HEAD))], [VMEM], "query"
-    )(queries.reshape(4, 2048))
+        query_kernel,
+        [shape((NZ, 64, HEAD)), shape((64, HEAD))],
+        [pl.BlockSpec(memory_space=pl.ANY)],
+        "query",
+        scratch=[pltpu.VMEM((4, 1, 2048), BF16), pltpu.SemaphoreType.DMA],
+    )(queries)
     near_queries = lax.all_to_all(
         query_rows.reshape(2 * NZ, 32, HEAD),
         PLANE,
@@ -392,16 +404,20 @@
         arrived = lax.ppermute(merged, PLANE, z_exchange(step))
         merged = call(pair_kernel, shape(PACKED), [VMEM] * 2, "pair")(merged, arrived)
     arrived = lax.ppermute(merged, PLANE, z_exchange(2))
-    product = call(
+    block = (NX, 4, 16, columns)
+    product, product_send = call(
         project_kernel,
-        shape((NX, 2, 4, 16, columns)),
-        [SMEM] * 2 + [VMEM] * 6,
+        [shape(block)] * 2,
+        [SMEM] + [VMEM] * 6,
         "project",
         flops=2 * 64 * 1024 * 640,
         moved=2 << 20,
-    )(x, core, merged, arrived, *weights)
+    )(x, merged, arrived, *weights)
+    product = call(add_kernel, shape(block), [VMEM] * 2, "add")(
+        product, lax.ppermute(product_send, "prefix", CORE_SWAP)
+    )
     terms = lax.all_to_all(
-        product.reshape(NX * 8, 16, columns),
+        product.reshape(NX * 4, 16, columns),
         PLANE + ("tensor",),
         0,
         0,

time: 86.8 us -> 86.6 us (level)
  blocking collectives: 17.1 us -> 12 us
  starting transfers between devices: 22.1 us -> 25.8 us
  waiting for transfers between devices: 18.2 us -> 19.2 us
    all_to_all x1, blocking collectives: 17.1 us -> 12 us  [local(): lax.all_to_all(product.reshape(NX * 4, 16, columns), PLANE + ('tensor',),...]
    ppermute x0 -> x1, starting transfers between devices: none -> 3.73 us  [local(): lax.ppermute(product_send, 'prefix', CORE_SWAP)]
    ppermute x0 -> x1, waiting for transfers between devices: none -> 0.9 us  [local(): lax.ppermute(product_send, 'prefix', CORE_SWAP)]
    unnamed x22 -> x21, local copies, waits for them, and re-layouts: 6.32 us -> 6.34 us
  transfers between devices with their start and end apart: 16 -> 17, of which waited for: 4 -> 5; matrix products, arithmetic and copies ran while one was open for 0% -> 0% of each run, Pallas kernels for 23% -> 23%
where the time goes in v3:
time: 86.6 us; the launch traced here: 86.1 us
  starting transfers between devices  25.8 us (30%)
  Pallas kernels  22 us (25%)
  waiting for transfers between devices  19.2 us (22%)
  blocking collectives  12 us (14%)
  local copies, waits for them, and re-layouts  6.34 us (7%)
    pallas_call x4, Pallas kernels, local(): attend(core, q, common_prefix_keys, common_prefix_values, other)  17 us
    all_to_all x1, blocking collectives, local(): lax.all_to_all(product.reshape(NX * 4, 16, columns), PLANE + ('tensor',),...  12 us
    all_to_all x1, starting transfers between devices, local(): lax.all_to_all(query_rows.reshape(2 * NZ, 32, HEAD), PLANE, 0, 0, tiled=T...  9.99 us
    ppermute x3, waiting for transfers between devices, local(): lax.ppermute(weight, 'replica', x_shift(-k))  8.03 us
    ppermute x2, waiting for transfers between devices, local(): arrived = lax.ppermute(merged, PLANE, z_exchange(step))  6.41 us
    unnamed x21, local copies, waits for them, and re-layouts  6.34 us
    ppermute x3, starting transfers between devices, local(): back = [lax.ppermute(partial[k], 'replica', x_shift(k)) for k in (1, 2, 3)]  3.99 us
    all_to_all x1, waiting for transfers between devices, local(): lax.all_to_all(query_rows.reshape(2 * NZ, 32, HEAD), PLANE, 0, 0, tiled=T...  3.79 us
  transfers between devices with their start and end apart: 17, of which 5 were waited for; matrix products, arithmetic and copies ran while one was open for 0% of the time, Pallas kernels for 23%

profile of v3, /device:TPU:1, one launch (start us, length us, event | category | flops | bytes accessed | tf_op | source)
XLA Modules:
  0.0 86.1 jit_solution(1597374591734777347)
XLA Ops:
  1.5 10.0 %all-to-all-start = ((bf16[16,32,128]{2,1,0:T(8,128)(2,1)}), bf16[16,32,128]{2,1,0:T(8,128)(2,1)S(1)}, u32[]{:S(2)}, u32[]{:S(2)}) async-start(bf16[16,32,128]{2,1,0:T(8,128)(2,1)} %bitcast.3), calls=%async_computation | async-start | bytes 262144 | tf_op jit(solution)/shard_map/all_to_all | solution.py:327
  11.5 1.4 %copy-done = bf16[3072,256]{1,0:T(8,128)(2,1)S(1)} copy-done((bf16[3072,256]{1,0:T(8,128)(2,1)S(1)}, bf16[3072,256]{1,0:T(8,128)(2,1)}, u32[]{:S(2)}) %copy-start) | copy-done | bytes 1572888
  12.9 1.4 %copy-done.2 = bf16[3072,256]{1,0:T(8,128)(2,1)S(1)} copy-done((bf16[3072,256]{1,0:T(8,128)(2,1)S(1)}, bf16[3072,256]{1,0:T(8,128)(2,1)}, u32[]{:S(2)}) %copy-start.2) | copy-done | bytes 1572888
  14.3 1.0 %copy-done.6 = bf16[2048,80]{0,1:T(8,128)(2,1)S(1)} copy-done((bf16[2048,80]{0,1:T(8,128)(2,1)S(1)}, bf16[2048,80]{0,1:T(8,128)(2,1)}, u32[]{:S(2)}) %copy-start.6) | copy-done | bytes 327704
  15.7 1.2 %copy-done.9 = bf16[3072,256]{1,0:T(8,128)(2,1)} copy-done((bf16[3072,256]{1,0:T(8,128)(2,1)}, bf16[3072,256]{1,0:T(8,128)(2,1)S(1)}, u32[]{:S(2)}) %copy-start.9) | copy-done | bytes 1572888
  16.9 3.8 %all-to-all-done = bf16[16,32,128]{2,1,0:T(8,128)(2,1)S(1)} async-done(((bf16[16,32,128]{2,1,0:T(8,128)(2,1)}), bf16[16,32,128]{2,1,0:T(8,128)(2,1)S(1)}, u32[]{:S(2)}, u32[]{:S(2)}) %all-to-all-start) | async-done | bytes 131104 | tf_op jit(solution)/shard_map/all_to_all | solution.py:327
  20.6 2.5 %collective-permute-start.1 = (bf16[8,64,128]{2,1,0:T(8,128)(2,1)S(1)}, bf16[8,64,128]{2,1,0:T(8,128)(2,1)S(1)}, u32[]{:S(2)}, u32[]{:S(2)}) collective-permute-start(bf16[8,64,128]{2,1,0:T(8,128)(2,1)S(1)} %bitcast.15), channel_id=1, source_target_pairs={{0,12},{4,0},{8,4},{12,8},{16,28},{20,16},{24,20},{28,24},{1,13},{... | collective-permute-start | bytes 393224 | tf_op jit(solution)/shard_map/ppermute | solution.py:394
  24.6 0.9 %collective-permute-start.7 = (f32[64,128]{1,0:T(8,128)S(1)}, f32[64,128]{1,0:T(8,128)S(1)}, u32[]{:S(2)}, u32[]{:S(2)}) collective-permute-start(f32[64,128]{1,0:T(8,128)S(1)} %get-tuple-element.22), channel_id=1, source_target_pairs={{0,32},{32,0},{64,96},{96,64},{128,160},{160,128},{192,224},{224,1... | collective-permute-start | bytes 98312 | tf_op jit(solution)/shard_map/ppermute | solution.py:381
  27.4 4.2 %attend.5 = bf16[528,128]{1,0:T(8,128)(2,1)S(1)} custom-call(s32[1]{0:T(128)} %bitcast.2.core_ref, bf16[8,64,128]{2,1,0:T(8,128)(2,1)S(1)} %collective-permute-done.1.q_ref, bf16[3072,256]{1,0:T(8,128)(2,1)S(1)} %copy-done.1, bf16[3072,256]{1,0:T(8,128)(2,1)S(1)} %copy-done.3, bf16[3072,256]{1,0:T(8,128)(2,1)S(1)} %fetch.1.other_ref), custom_call_target="tpu_custom_call" | custom-call | flops 1610612736 | bytes 4718592 | tf_op jit(solution)/shard_map/attend/pallas_call | solution.py:397
  31.6 1.2 %collective-permute-start.2 = (bf16[528,128]{1,0:T(8,128)(2,1)S(1)}, bf16[528,128]{1,0:T(8,128)(2,1)S(1)}, u32[]{:S(2)}, u32[]{:S(2)}) collective-permute-start(bf16[528,128]{1,0:T(8,128)(2,1)S(1)} %attend.5), channel_id=1, source_target_pairs={{0,4},{4,8},{8,12},{12,0},{16,20},{20,24},{24,28},{28,16},{1,5},{5... | collective-permute-start | bytes 405512 | tf_op jit(solution)/shard_map/ppermute | solution.py:399
  32.8 4.4 %attend.6 = bf16[528,128]{1,0:T(8,128)(2,1)S(1)} custom-call(s32[1]{0:T(128)} %bitcast.2.core_ref, bf16[8,64,128]{2,1,0:T(8,128)(2,1)S(1)} %collective-permute-done.3.q_ref, bf16[3072,256]{1,0:T(8,128)(2,1)S(1)} %copy-done.1, bf16[3072,256]{1,0:T(8,128)(2,1)S(1)} %copy-done.3, bf16[3072,256]{1,0:T(8,128)(2,1)S(1)} %fetch.1.other_ref), custom_call_target="tpu_custom_call" | custom-call | flops 1610612736 | bytes 4718592 | tf_op jit(solution)/shard_map/attend/pallas_call | solution.py:397
  37.2 1.8 %collective-permute-start.4 = (bf16[528,128]{1,0:T(8,128)(2,1)S(1)}, bf16[528,128]{1,0:T(8,128)(2,1)S(1)}, u32[]{:S(2)}, u32[]{:S(2)}) collective-permute-start(bf16[528,128]{1,0:T(8,128)(2,1)S(1)} %attend.6), channel_id=1, source_target_pairs={{0,8},{4,12},{8,0},{12,4},{16,24},{20,28},{24,16},{28,20},{1,9},{5... | collective-permute-start | bytes 405512 | tf_op jit(solution)/shard_map/ppermute | solution.py:399
  39.0 4.2 %attend.7 = bf16[528,128]{1,0:T(8,128)(2,1)S(1)} custom-call(s32[1]{0:T(128)} %bitcast.2.core_ref, bf16[8,64,128]{2,1,0:T(8,128)(2,1)S(1)} %collective-permute-done.5.q_ref, bf16[3072,256]{1,0:T(8,128)(2,1)S(1)} %copy-done.1, bf16[3072,256]{1,0:T(8,128)(2,1)S(1)} %copy-done.3, bf16[3072,256]{1,0:T(8,128)(2,1)S(1)} %fetch.1.other_ref), custom_call_target="tpu_custom_call" | custom-call | flops 1610612736 | bytes 4718592 | tf_op jit(solution)/shard_map/attend/pallas_call | solution.py:397
  43.2 1.0 %collective-permute-start.6 = (bf16[528,128]{1,0:T(8,128)(2,1)S(1)}, bf16[528,128]{1,0:T(8,128)(2,1)S(1)}, u32[]{:S(2)}, u32[]{:S(2)}) collective-permute-start(bf16[528,128]{1,0:T(8,128)(2,1)S(1)} %attend.7), channel_id=1, source_target_pairs={{0,12},{4,0},{8,4},{12,8},{16,28},{20,16},{24,20},{28,24},{1,13},{... | collective-permute-start | bytes 405512 | tf_op jit(solution)/shard_map/ppermute | solution.py:399
  44.2 4.2 %attend.4.a_ref = bf16[528,128]{1,0:T(8,128)(2,1)S(1)} custom-call(s32[1]{0:T(128)} %bitcast.2.core_ref, bf16[8,64,128]{2,1,0:T(8,128)(2,1)S(1)} %bitcast.18, bf16[3072,256]{1,0:T(8,128)(2,1)S(1)} %copy-done.1, bf16[3072,256]{1,0:T(8,128)(2,1)S(1)} %copy-done.3, bf16[3072,256]{1,0:T(8,128)(2,1)S(1)} %fetch.1.other_ref), custom_call_target="tpu_custom_call" | custom-call | flops 1610612736 | bytes 4718592 | tf_op jit(solution)/shard_map/attend/pallas_call | solution.py:397
  48.4 1.0 %merge.1.a_ref = bf16[528,128]{1,0:T(8,128)(2,1)S(1)} custom-call(s32[1]{0:T(128)} %bitcast.1.z_ref, s32[1]{0:T(128)} %bitcast.2.core_ref, bf16[528,128]{1,0:T(8,128)(2,1)S(1)} %attend.4.a_ref, bf16[528,128]{1,0:T(8,128)(2,1)S(1)} %collective-permute-done.2.b_ref, bf16[528,128]{1,0:T(8,128)(2,1)S(1)} %collective-permute-done.4.c_ref, ...), custom_call_target="tpu_custom_call" | custom-call | bytes 811008 | tf_op jit(solution)/shard_map/merge/pallas_call | solution.py:400
  49.6 0.9 %collective-permute-start.12 = (bf16[160,1024]{1,0:T(8,128)(2,1)S(1)}, bf16[160,1024]{1,0:T(8,128)(2,1)S(1)}, u32[]{:S(2)}, u32[]{:S(2)}) collective-permute-start(bf16[160,1024]{1,0:T(8,128)(2,1)S(1)} %stack.1.refs_0_), channel_id=1, source_target_pairs={{0,12},{4,0},{8,4},{12,8},{16,28},{20,16},{24,20},{28,24},{1,13},{... | collective-permute-start | bytes 983048 | tf_op jit(solution)/shard_map/ppermute | solution.py:362
  50.5 1.7 %collective-permute-start.13 = (bf16[160,1024]{1,0:T(8,128)(2,1)S(1)}, bf16[160,1024]{1,0:T(8,128)(2,1)S(1)}, u32[]{:S(2)}, u32[]{:S(2)}) collective-permute-start(bf16[160,1024]{1,0:T(8,128)(2,1)S(1)} %stack.1.refs_0_), channel_id=1, source_target_pairs={{0,8},{4,12},{8,0},{12,4},{16,24},{20,28},{24,16},{28,20},{1,9},{5... | collective-permute-start | bytes 983048 | tf_op jit(solution)/shard_map/ppermute | solution.py:362
  52.3 1.1 %collective-permute-done.8.b_ref = bf16[528,128]{1,0:T(8,128)(2,1)S(1)} collective-permute-done((bf16[528,128]{1,0:T(8,128)(2,1)S(1)}, bf16[528,128]{1,0:T(8,128)(2,1)S(1)}, u32[]{:S(2)}, u32[]{:S(2)}) %collective-permute-start.8) | collective-permute-done | bytes 135200 | tf_op jit(solution)/shard_map/ppermute | solution.py:404
  53.8 5.3 %collective-permute-done.9.b_ref = bf16[528,128]{1,0:T(8,128)(2,1)S(1)} collective-permute-done((bf16[528,128]{1,0:T(8,128)(2,1)S(1)}, bf16[528,128]{1,0:T(8,128)(2,1)S(1)}, u32[]{:S(2)}, u32[]{:S(2)}) %collective-permute-start.9) | collective-permute-done | bytes 135200 | tf_op jit(solution)/shard_map/ppermute | solution.py:404
  60.0 8.0 %collective-permute-done.14.refs_3_ = bf16[160,1024]{1,0:T(8,128)(2,1)S(1)} collective-permute-done((bf16[160,1024]{1,0:T(8,128)(2,1)S(1)}, bf16[160,1024]{1,0:T(8,128)(2,1)S(1)}, u32[]{:S(2)}, u32[]{:S(2)}) %collective-permute-start.14) | collective-permute-done | bytes 327712 | tf_op jit(solution)/shard_map/ppermute | solution.py:362
  68.7 3.7 %collective-permute-start.15 = (bf16[4,4,16,80]{3,2,1,0:T(8,128)(2,1)S(1)}, bf16[4,4,16,80]{3,2,1,0:T(8,128)(2,1)S(1)}, u32[]{:S(2)}, u32[]{:S(2)}) collective-permute-start(bf16[4,4,16,80]{3,2,1,0:T(8,128)(2,1)S(1)} %get-tuple-element.26), channel_id=1, source_target_pairs={{0,32},{32,0},{64,96},{96,64},{128,160},{160,128},{192,224},{224,1... | collective-permute-start | bytes 122888 | tf_op jit(solution)/shard_map/ppermute | solution.py:417
  72.4 0.9 %collective-permute-done.15.b_ref = bf16[4,4,16,80]{3,2,1,0:T(8,128)(2,1)S(1)} collective-permute-done((bf16[4,4,16,80]{3,2,1,0:T(8,128)(2,1)S(1)}, bf16[4,4,16,80]{3,2,1,0:T(8,128)(2,1)S(1)}, u32[]{:S(2)}, u32[]{:S(2)}) %collective-permute-start.15) | collective-permute-done | bytes 40992 | tf_op jit(solution)/shard_map/ppermute | solution.py:417
  73.3 12.0 %all_to_all.10.terms_ref = bf16[16,16,80]{2,1,0:T(8,128)(2,1)S(1)} all-to-all(bf16[16,16,80]{2,1,0:T(8,128)(2,1)S(1)} %bitcast.14), channel_id=1, replica_groups={{0,1,2,3,4,5,6,7,8,9,10,11,12,13,14,15},{32,33,34,35,36,37,38,39,40,41,..., dimensions={0} | all-to-all | bytes 81920 | tf_op jit(solution)/shard_map/all_to_all | solution.py:419
  (47 shorter events, 7.6 us)
Async XLA Ops:
  1.5 19.2 %all-to-all-start = ((bf16[16,32,128]{2,1,0:T(8,128)(2,1)}), bf16[16,32,128]{2,1,0:T(8,128)(2,1)S(1)}, u32[]{:S(2)}, u32[]{:S(2)}) async-start(bf16[16,32,128]{2,1,0:T(8,128)(2,1)} %bitcast.3), calls=%async_computation | async-start | bytes 262144 | tf_op jit(solution)/shard_map/all_to_all | solution.py:327
  11.5 1.4 %copy-start = (bf16[3072,256]{1,0:T(8,128)(2,1)S(1)}, bf16[3072,256]{1,0:T(8,128)(2,1)}, u32[]{:S(2)}) copy-start(bf16[3072,256]{1,0:T(8,128)(2,1)} %k_ref.9) | copy-start | bytes 4718596
  12.9 1.4 %copy-start.2 = (bf16[3072,256]{1,0:T(8,128)(2,1)S(1)}, bf16[3072,256]{1,0:T(8,128)(2,1)}, u32[]{:S(2)}) copy-start(bf16[3072,256]{1,0:T(8,128)(2,1)} %v_ref.9) | copy-start | bytes 4718596
  15.3 8.5 %copy-start.4 = (bf16[1,1024,256]{2,1,0:T(8,128)(2,1)S(1)}, bf16[1,1024,256]{2,1,0:T(8,128)(2,1)}, u32[]{:S(2)}) copy-start(bf16[1,1024,256]{2,1,0:T(8,128)(2,1)} %param.12) | copy-start | bytes 1572868
  15.3 8.5 %copy-start.5 = (bf16[1,1024,256]{2,1,0:T(8,128)(2,1)S(1)}, bf16[1,1024,256]{2,1,0:T(8,128)(2,1)}, u32[]{:S(2)}) copy-start(bf16[1,1024,256]{2,1,0:T(8,128)(2,1)} %param.13) | copy-start | bytes 1572868
  15.3 8.5 %copy-start.7 = (bf16[4,1,256]{2,0,1:T(4,128)(2,1)S(1)}, bf16[4,1,256]{2,0,1:T(4,128)(2,1)}, u32[]{:S(2)}) copy-start(bf16[4,1,256]{2,0,1:T(4,128)(2,1)} %param.14) | copy-start | bytes 6148
  15.3 8.5 %copy-start.8 = (bf16[4,1,256]{2,0,1:T(4,128)(2,1)S(1)}, bf16[4,1,256]{2,0,1:T(4,128)(2,1)}, u32[]{:S(2)}) copy-start(bf16[4,1,256]{2,0,1:T(4,128)(2,1)} %param.15) | copy-start | bytes 6148
  20.6 5.4 %collective-permute-start = (bf16[3072,256]{1,0:T(8,128)(2,1)}, bf16[3072,256]{1,0:T(8,128)(2,1)S(1)}, u32[]{:S(2)}, u32[]{:S(2)}) collective-permute-start(bf16[3072,256]{1,0:T(8,128)(2,1)} %copy-done.9), channel_id=1, source_target_pairs={{0,32},{32,0},{64,96},{96,64},{128,160},{160,128},{192,224},{224,1... | collective-permute-start | bytes 4718600 | tf_op jit(solution)/shard_map/ppermute | solution.py:357
  20.6 6.2 %collective-permute-start.1 = (bf16[8,64,128]{2,1,0:T(8,128)(2,1)S(1)}, bf16[8,64,128]{2,1,0:T(8,128)(2,1)S(1)}, u32[]{:S(2)}, u32[]{:S(2)}) collective-permute-start(bf16[8,64,128]{2,1,0:T(8,128)(2,1)S(1)} %bitcast.15), channel_id=1, source_target_pairs={{0,12},{4,0},{8,4},{12,8},{16,28},{20,16},{24,20},{28,24},{1,13},{... | collective-permute-start | bytes 393224 | tf_op jit(solution)/shard_map/ppermute | solution.py:394
  24.6 23.8 %collective-permute-start.7 = (f32[64,128]{1,0:T(8,128)S(1)}, f32[64,128]{1,0:T(8,128)S(1)}, u32[]{:S(2)}, u32[]{:S(2)}) collective-permute-start(f32[64,128]{1,0:T(8,128)S(1)} %get-tuple-element.22), channel_id=1, source_target_pairs={{0,32},{32,0},{64,96},{96,64},{128,160},{160,128},{192,224},{224,1... | collective-permute-start | bytes 98312 | tf_op jit(solution)/shard_map/ppermute | solution.py:381
  25.5 24.1 %collective-permute-start.11 = (bf16[80,1024]{1,0:T(8,128)(2,1)S(1)}, bf16[80,1024]{1,0:T(8,128)(2,1)S(1)}, u32[]{:S(2)}, u32[]{:S(2)}) collective-permute-start(bf16[80,1024]{1,0:T(8,128)(2,1)S(1)} %get-tuple-element.24), channel_id=1, source_target_pairs={{0,32},{32,0},{64,96},{96,64},{128,160},{160,128},{192,224},{224,1... | collective-permute-start | bytes 491528 | tf_op jit(solution)/shard_map/ppermute | solution.py:360
  25.6 1.9 %copy-start.3 = (bf16[3072,256]{1,0:T(8,128)(2,1)S(1)}, bf16[3072,256]{1,0:T(8,128)(2,1)}, u32[]{:S(2)}) copy-start(bf16[3072,256]{1,0:T(8,128)(2,1)} %v_ref.9) | copy-start | bytes 4718596
  25.6 7.3 %collective-permute-start.3 = (bf16[8,64,128]{2,1,0:T(8,128)(2,1)S(1)}, bf16[8,64,128]{2,1,0:T(8,128)(2,1)S(1)}, u32[]{:S(2)}, u32[]{:S(2)}) collective-permute-start(bf16[8,64,128]{2,1,0:T(8,128)(2,1)S(1)} %bitcast.16), channel_id=1, source_target_pairs={{0,8},{4,12},{8,0},{12,4},{16,24},{20,28},{24,16},{28,20},{1,9},{5... | collective-permute-start | bytes 393224 | tf_op jit(solution)/shard_map/ppermute | solution.py:394
  26.1 12.9 %collective-permute-start.5 = (bf16[8,64,128]{2,1,0:T(8,128)(2,1)S(1)}, bf16[8,64,128]{2,1,0:T(8,128)(2,1)S(1)}, u32[]{:S(2)}, u32[]{:S(2)}) collective-permute-start(bf16[8,64,128]{2,1,0:T(8,128)(2,1)S(1)} %bitcast.17), channel_id=1, source_target_pairs={{0,4},{4,8},{8,12},{12,0},{16,20},{20,24},{24,28},{28,16},{1,5},{5... | collective-permute-start | bytes 393224 | tf_op jit(solution)/shard_map/ppermute | solution.py:394
  31.6 16.8 %collective-permute-start.2 = (bf16[528,128]{1,0:T(8,128)(2,1)S(1)}, bf16[528,128]{1,0:T(8,128)(2,1)S(1)}, u32[]{:S(2)}, u32[]{:S(2)}) collective-permute-start(bf16[528,128]{1,0:T(8,128)(2,1)S(1)} %attend.5), channel_id=1, source_target_pairs={{0,4},{4,8},{8,12},{12,0},{16,20},{20,24},{24,28},{28,16},{1,5},{5... | collective-permute-start | bytes 405512 | tf_op jit(solution)/shard_map/ppermute | solution.py:399
  37.2 11.2 %collective-permute-start.4 = (bf16[528,128]{1,0:T(8,128)(2,1)S(1)}, bf16[528,128]{1,0:T(8,128)(2,1)S(1)}, u32[]{:S(2)}, u32[]{:S(2)}) collective-permute-start(bf16[528,128]{1,0:T(8,128)(2,1)S(1)} %attend.6), channel_id=1, source_target_pairs={{0,8},{4,12},{8,0},{12,4},{16,24},{20,28},{24,16},{28,20},{1,9},{5... | collective-permute-start | bytes 405512 | tf_op jit(solution)/shard_map/ppermute | solution.py:399
  43.2 5.2 %collective-permute-start.6 = (bf16[528,128]{1,0:T(8,128)(2,1)S(1)}, bf16[528,128]{1,0:T(8,128)(2,1)S(1)}, u32[]{:S(2)}, u32[]{:S(2)}) collective-permute-start(bf16[528,128]{1,0:T(8,128)(2,1)S(1)} %attend.7), channel_id=1, source_target_pairs={{0,12},{4,0},{8,4},{12,8},{16,28},{20,16},{24,20},{28,24},{1,13},{... | collective-permute-start | bytes 405512 | tf_op jit(solution)/shard_map/ppermute | solution.py:399
  49.4 3.9 %collective-permute-start.8 = (bf16[528,128]{1,0:T(8,128)(2,1)S(1)}, bf16[528,128]{1,0:T(8,128)(2,1)S(1)}, u32[]{:S(2)}, u32[]{:S(2)}) collective-permute-start(bf16[528,128]{1,0:T(8,128)(2,1)S(1)} %merge.1.a_ref), channel_id=1, source_target_pairs={{0,16},{32,48},{16,0},{48,32},{64,80},{96,112},{80,64},{112,96},{1... | collective-permute-start | bytes 405512 | tf_op jit(solution)/shard_map/ppermute | solution.py:404
  49.6 10.4 %collective-permute-start.12 = (bf16[160,1024]{1,0:T(8,128)(2,1)S(1)}, bf16[160,1024]{1,0:T(8,128)(2,1)S(1)}, u32[]{:S(2)}, u32[]{:S(2)}) collective-permute-start(bf16[160,1024]{1,0:T(8,128)(2,1)S(1)} %stack.1.refs_0_), channel_id=1, source_target_pairs={{0,12},{4,0},{8,4},{12,8},{16,28},{20,16},{24,20},{28,24},{1,13},{... | collective-permute-start | bytes 983048 | tf_op jit(solution)/shard_map/ppermute | solution.py:362
  50.5 9.5 %collective-permute-start.13 = (bf16[160,1024]{1,0:T(8,128)(2,1)S(1)}, bf16[160,1024]{1,0:T(8,128)(2,1)S(1)}, u32[]{:S(2)}, u32[]{:S(2)}) collective-permute-start(bf16[160,1024]{1,0:T(8,128)(2,1)S(1)} %stack.1.refs_0_), channel_id=1, source_target_pairs={{0,8},{4,12},{8,0},{12,4},{16,24},{20,28},{24,16},{28,20},{1,9},{5... | collective-permute-start | bytes 983048 | tf_op jit(solution)/shard_map/ppermute | solution.py:362
  52.3 15.8 %collective-permute-start.14 = (bf16[160,1024]{1,0:T(8,128)(2,1)S(1)}, bf16[160,1024]{1,0:T(8,128)(2,1)S(1)}, u32[]{:S(2)}, u32[]{:S(2)}) collective-permute-start(bf16[160,1024]{1,0:T(8,128)(2,1)S(1)} %stack.1.refs_0_), channel_id=1, source_target_pairs={{0,4},{4,8},{8,12},{12,0},{16,20},{20,24},{24,28},{28,16},{1,5},{5... | collective-permute-start | bytes 983048 | tf_op jit(solution)/shard_map/ppermute | solution.py:362
  53.7 5.5 %collective-permute-start.9 = (bf16[528,128]{1,0:T(8,128)(2,1)S(1)}, bf16[528,128]{1,0:T(8,128)(2,1)S(1)}, u32[]{:S(2)}, u32[]{:S(2)}) collective-permute-start(bf16[528,128]{1,0:T(8,128)(2,1)S(1)} %pair.2.a_ref), channel_id=1, source_target_pairs={{0,208},{32,240},{16,64},{48,96},{64,16},{96,48},{80,128},{112,160... | collective-permute-start | bytes 405512 | tf_op jit(solution)/shard_map/ppermute | solution.py:404
  59.5 8.6 %collective-permute-start.10 = (bf16[528,128]{1,0:T(8,128)(2,1)S(1)}, bf16[528,128]{1,0:T(8,128)(2,1)S(1)}, u32[]{:S(2)}, u32[]{:S(2)}) collective-permute-start(bf16[528,128]{1,0:T(8,128)(2,1)S(1)} %pair.3.a_ref), channel_id=1, source_target_pairs={{0,80},{32,112},{16,192},{48,224},{64,144},{96,176},{80,0},{112,32... | collective-permute-start | bytes 405512 | tf_op jit(solution)/shard_map/ppermute | solution.py:406
  68.7 4.6 %collective-permute-start.15 = (bf16[4,4,16,80]{3,2,1,0:T(8,128)(2,1)S(1)}, bf16[4,4,16,80]{3,2,1,0:T(8,128)(2,1)S(1)}, u32[]{:S(2)}, u32[]{:S(2)}) collective-permute-start(bf16[4,4,16,80]{3,2,1,0:T(8,128)(2,1)S(1)} %get-tuple-element.26), channel_id=1, source_target_pairs={{0,32},{32,0},{64,96},{96,64},{128,160},{160,128},{192,224},{224,1... | collective-permute-start | bytes 122888 | tf_op jit(solution)/shard_map/ppermute | solution.py:417
  (3 other events, 3.6 us)
